TPU v7x, 128 devices: a whole 4x4x4 slice. The times are simulated.
128 devices in a mesh: views: 16 (over x, y), sub: 8 (over z, core).
Axes of the slice: x: 4, y: 4, z: 4, core: 2. Of those that a mesh axis runs over, the one named last changes fastest.
Arguments:
- queries: bfloat16 [32768, 512], P(('views', 'sub')), may hold values from -300 to 300
- keys: bfloat16 [32768, 512], P(('views', 'sub')), may hold values from -7 to 7
- values: bfloat16 [32768, 512], P(('views', 'sub')), may hold values from -6 to 6
- out_grad: bfloat16 [32768, 512], P(('views', 'sub')), may hold values from -6 to 6
- block_lists: int32 [256, 16], P(('views', 'sub')), may hold values from -1 to 255, as said below
Outputs:
- query_grad: bfloat16 [32768, 512], P(('views', 'sub'))
- key_grad: bfloat16 [32768, 512], P(('views', 'sub'))
- value_grad: bfloat16 [32768, 512], P(('views', 'sub'))
Inputs may be any that keep to these rules, and one draw needn't show every extreme that they name: `block_lists`: an entry is -1 (no block) or the number of a key block of another view that lies at the same band position, sub index, as the query block; the entries of one query block are distinct. Of all entries of the 2 query blocks of one band of one view, at most 1 name blocks of any one view, and exactly 1 name blocks of some view.
All inputs are finite; a program needn't handle non-finite values.
Results may differ from a plain program's by a relative error of at most 0.0075.
Values may be sent and summed in bfloat16 or wider, within the bound.
A program may use at most 192 MiB of HBM per device.

v0:
```python
import jax
import jax.numpy as jnp
from jax import lax
from jax.sharding import PartitionSpec as P

HEADS = 8
CAP = 1


masked_score = -1e30


def passed_along(x, axis, by):
    length = lax.axis_size(axis)
    pairs = [(i, i + by) for i in range(length) if 0 <= i + by < length]
    return lax.ppermute(x, axis, pairs)


def block_backward(query_blk, grad_blk, key_set, value_set, usable):
    head_size = query_blk.shape[-1]
    scaling = head_size ** (-0.5)
    scores = (
        jnp.einsum("ihd,kjhd->hikj", query_blk, key_set, preferred_element_type=jnp.float32)
        * scaling
    )
    scores = jnp.where(usable[None, None, :, None], scores, masked_score)
    row_max = jnp.max(scores, axis=(2, 3), keepdims=True)
    raised = jnp.exp(scores - row_max)
    attn_prob = raised / jnp.sum(raised, axis=(2, 3), keepdims=True)
    rounded = attn_prob.astype(jnp.bfloat16)
    attended = jnp.einsum("hikj,kjhd->ihd", rounded, value_set, preferred_element_type=jnp.float32)
    row_delta = jnp.sum(grad_blk.astype(jnp.float32) * attended, axis=2)
    prob_grad = jnp.einsum(
        "ihd,kjhd->hikj", grad_blk, value_set, preferred_element_type=jnp.float32
    )
    score_grad = (
        attn_prob * (prob_grad - jnp.transpose(row_delta)[:, :, None, None]) * scaling
    ).astype(jnp.bfloat16)
    query_part = jnp.einsum(
        "hikj,kjhd->ihd", score_grad, key_set, preferred_element_type=jnp.float32
    )
    key_part = jnp.einsum(
        "hikj,ihd->kjhd", score_grad, query_blk, preferred_element_type=jnp.float32
    )
    value_part = jnp.einsum("hikj,ihd->kjhd", rounded, grad_blk, preferred_element_type=jnp.float32)
    return (query_part, key_part, value_part)


def shards(queries, keys, values, out_grad, block_lists):
    token_rows, feature_width = queries.shape
    block_count, list_slots = block_lists.shape
    block_rows = token_rows // block_count
    head_count = HEADS
    head_size = feature_width // head_count
    view_count = lax.axis_size("views")
    band_index = lax.axis_index("sub")
    per_view = lax.axis_size("sub") * block_count
    stacked = jnp.stack([keys, values])
    before = passed_along(stacked[:, token_rows - block_rows :], "sub", 1)
    extended = jnp.concatenate([before, stacked], axis=1).reshape(
        2, block_count + 1, block_rows, feature_width
    )
    blocks = stacked.reshape(2, block_count, block_rows, feature_width)
    flat_ids = block_lists.reshape(-1)
    is_live = flat_ids >= 0
    safe_ids = jnp.where(is_live, flat_ids, 0)
    owners = safe_ids // per_view
    local_blk = safe_ids % block_count
    entry_count = flat_ids.shape[0]
    owner_hits = ((owners[:, None] == jnp.arange(view_count)[None, :]) & is_live[:, None]).astype(
        jnp.int32
    )
    before_count = jnp.cumsum(owner_hits, axis=0) - owner_hits
    slot_rank = jnp.sum(before_count * owner_hits, axis=1)
    slot_hit = owner_hits[:, :, None] * (
        slot_rank[:, None, None] == jnp.arange(CAP)[None, None, :]
    ).astype(jnp.int32)
    request = jnp.sum(slot_hit * (local_blk + 1)[:, None, None], axis=0) - 1
    wanted = lax.all_to_all(request, "views", split_axis=0, concat_axis=0, tiled=True)
    offered = blocks[:, jnp.maximum(wanted, 0)]
    fetched = lax.all_to_all(offered, "views", split_axis=1, concat_axis=1, tiled=True)
    position = owners * CAP + slot_rank
    picked = fetched.reshape(2, view_count * CAP, block_rows, feature_width)[:, position]
    picked = picked.reshape(2, block_count, list_slots, block_rows, feature_width)
    window = jnp.stack([extended[:, :block_count], extended[:, 1:]], axis=2)
    key_sets = jnp.concatenate([window, picked], axis=2)
    set_size = list_slots + 2
    prev_ok = (jnp.arange(block_count) > 0) | (band_index > 0)
    usable = jnp.concatenate(
        [
            prev_ok[:, None],
            jnp.ones((block_count, 1), bool),
            is_live.reshape(block_count, list_slots),
        ],
        axis=1,
    )

    def per_block(piece_set):
        query_blk, grad_blk, key_set, value_set, usable_row = piece_set
        return block_backward(
            query_blk.reshape(block_rows, head_count, head_size),
            grad_blk.reshape(block_rows, head_count, head_size),
            key_set.reshape(set_size, block_rows, head_count, head_size),
            value_set.reshape(set_size, block_rows, head_count, head_size),
            usable_row,
        )

    query_part, key_part, value_part = lax.map(
        per_block,
        (
            queries.reshape(block_count, block_rows, feature_width),
            out_grad.reshape(block_count, block_rows, feature_width),
            key_sets[0],
            key_sets[1],
            usable,
        ),
    )
    query_grad = query_part.reshape(token_rows, feature_width).astype(jnp.bfloat16)
    gradients = jnp.stack(
        [
            key_part.reshape(block_count, set_size, block_rows, feature_width),
            value_part.reshape(block_count, set_size, block_rows, feature_width),
        ]
    )
    zero_block = jnp.zeros((2, 1, block_rows, feature_width), jnp.float32)
    local_sum = gradients[:, :, 1] + jnp.concatenate([gradients[:, 1:, 0], zero_block], axis=1)
    returned = passed_along(gradients[:, 0, 0], "sub", -1)
    local_sum = local_sum + jnp.concatenate(
        [
            jnp.zeros((2, block_count - 1, block_rows, feature_width), jnp.float32),
            returned[:, None],
        ],
        axis=1,
    )
    entry_grads = gradients[:, :, 2:].reshape(2, entry_count, block_rows, feature_width)
    chooser = slot_hit.reshape(entry_count, view_count * CAP).astype(jnp.float32)
    outgoing = jnp.einsum("es,xejw->xsjw", chooser, entry_grads, precision=lax.Precision.HIGHEST)
    outgoing = outgoing.reshape(2, view_count, CAP, block_rows, feature_width)
    arrived = lax.all_to_all(outgoing, "views", split_axis=1, concat_axis=1, tiled=True)
    owner_match = (wanted.reshape(-1)[:, None] == jnp.arange(block_count)[None, :]).astype(
        jnp.float32
    )
    remote = jnp.einsum(
        "sb,xsjw->xbjw",
        owner_match,
        arrived.reshape(2, view_count * CAP, block_rows, feature_width),
        precision=lax.Precision.HIGHEST,
    )
    summed = (local_sum + remote).reshape(2, token_rows, feature_width)
    return (query_grad, summed[0].astype(jnp.bfloat16), summed[1].astype(jnp.bfloat16))


def solution(mesh):
    in_specs = (
        P(("views", "sub"), None),
        P(("views", "sub"), None),
        P(("views", "sub"), None),
        P(("views", "sub"), None),
        P(("views", "sub"), None),
    )
    out_specs = (P(("views", "sub"), None), P(("views", "sub"), None), P(("views", "sub"), None))
    return jax.shard_map(shards, mesh=mesh, in_specs=in_specs, out_specs=out_specs, check_vma=False)
```

profile of v0, /device:TPU:92, one launch (start us, length us, event | category | flops | bytes accessed | tf_op | source)
XLA Modules:
  0.0 358.2 jit_solution(13186823043108677221)
XLA Ops:
  0.6 0.8 reshape.356
  1.7 0.5 copy-done.14
  2.3 0.7 copy.167
  3.0 7.1 %all-to-all-start = ((s32[16,1,1]{2,1,0:T(1,128)}), s32[16,1,1]{2,1,0:T(1,128)S(1)}, u32[]{:S(2)}, u32[]{:S(2)}) async-start(s32[16,1,1]{2,1,0:T(1,128)} %copy.167), calls=%async_computation | async-start | bytes 16384 | tf_op jit(solution)/shard_map/all_to_all | solution.py:79
  10.1 1.1 pad_maximum_fusion.2
  11.2 2.6 all-to-all-done
  13.8 1.0 fusion.58
  14.9 2.8 gather_fusion
  17.7 8.2 %all-to-all-start.1 = ((bf16[2,16,1,128,512]{4,3,0,2,1:T(8,128)(2,1)}), bf16[2,16,1,128,512]{4,3,0,2,1:T(8,128)(2,1)}, u32[]{:S(2)}, u32[]{:S(2)}) async-start(bf16[2,16,1,128,512]{4,3,0,2,1:T(8,128)(2,1)} %bitcast.175), calls=%async_computation.1 | async-start | bytes 8388608 | tf_op jit(solution)/shard_map/all_to_all | solution.py:81
  25.9 1.9 collective-permute-start
  28.2 5.4 %collective-permute-done = bf16[2,128,512]{2,1,0:T(8,128)(2,1)S(1)} collective-permute-done((bf16[2,128,512]{2,1,0:T(8,128)(2,1)S(1)}, bf16[2,128,512]{2,1,0:T(8,128)(2,1)S(1)}, u32[]{:S(2)}, u32[]{:S(2)}) %collective-permute-start) | collective-permute-done | bytes 262176 | tf_op jit(solution)/shard_map/ppermute | solution.py:16
  33.8 1.0 copy.170
  34.8 1.0 copy.171
  35.8 42.6 %all-to-all-done.1 = bf16[2,16,1,128,512]{4,3,0,2,1:T(8,128)(2,1)} async-done(((bf16[2,16,1,128,512]{4,3,0,2,1:T(8,128)(2,1)}), bf16[2,16,1,128,512]{4,3,0,2,1:T(8,128)(2,1)}, u32[]{:S(2)}, u32[]{:S(2)}) %all-to-all-start.1) | async-done | bytes 4194336 | tf_op jit(solution)/shard_map/all_to_all | solution.py:81
  78.3 4.7 %copy.246 = bf16[2,16,1,128,512]{4,3,1,0,2:T(8,128)(2,1)} copy(bf16[2,16,1,128,512]{4,3,0,2,1:T(8,128)(2,1)} %all-to-all-done.1) | data formatting | bytes 8388608 | tf_op jit(solution)/shard_map/all_to_all | solution.py:81
  83.0 7.1 %gather_fusion.1 = bf16[32,2,128,512]{3,2,1,0:T(8,128)(2,1)} fusion(bf16[2,16,128,512]{3,2,1,0:T(8,128)(2,1)} %bitcast.171, s32[1024]{0:T(1024)S(1)} %pad_clamp_fusion), kind=kCustom, calls=%fused_computation.1 | custom fusion | bytes 16777344 | tf_op jit(solution)/shard_map/gather | solution.py:83
  90.1 11.4 %copy.172 = bf16[2,2,16,128,512]{3,4,2,1,0:T(8,128)(2,1)} copy(bf16[2,2,16,128,512]{4,3,0,2,1:T(8,128)(2,1)} %bitcast.172) | data formatting | bytes 16777216 | tf_op jit(solution)/shard_map/reshape | solution.py:84
  101.4 5.2 %pad_maximum_fusion.1 = bf16[2,2,18,128,512]{3,4,2,1,0:T(8,128)(2,1)S(1)} fusion(bf16[2,2,16,128,512]{3,4,2,1,0:T(8,128)(2,1)} %copy.172, bf16[2,2,1,128,512]{3,4,2,1,0:T(8,128)(2,1)} %copy.171, bf16[2,2,1,128,512]{3,4,2,1,0:T(8,128)(2,1)} %copy.170), kind=kLoop, calls=%fused_computation.32 | loop fusion | flops 9437184 | bytes 18874368 | tf_op jit(solution)/shard_map/concatenate | solution.py:86
  106.7 4.8 %slice_bitcast_fusion = (bf16[2,18,128,512]{2,3,1,0:T(8,128)(2,1)}, bf16[2,18,128,512]{2,3,1,0:T(8,128)(2,1)}) fusion(bf16[2,2,18,128,512]{3,4,2,1,0:T(8,128)(2,1)S(1)} %pad_maximum_fusion.1), kind=kLoop, calls=%fused_computation.36 | loop fusion | bytes 18874368 | tf_op jit(solution)/shard_map/squeeze | solution.py:114
  111.5 56.7 %while.14 = (s32[]{:T(128)}, bf16[2,128,8,64]{1,3,2,0:T(8,128)(2,1)}, f32[2,18,128,8,64]{2,4,3,1,0:T(8,128)}, f32[2,18,128,8,64]{2,4,3,1,0:T(8,128)}, bf16[2,18,...) while((s32[]{:T(128)}, ...), condition=%wide.region_7.8_spmd, body=%wide.region_3.7_spmd.sunk | while | flops 1859318784 | bytes 155095456 | solution.py:108
  112.0 0.9 constant_dynamic-slice_fusion.12
  113.2 1.8 constant_dynamic-slice_fusion.10
  115.0 2.7 constant_dynamic-slice_fusion.9
  117.7 1.5 copy-done
  119.2 2.1 fusion.98
  121.3 1.9 fusion.99
  123.2 2.4 fusion.100
  125.7 1.1 fusion.101
  126.7 1.7 convolution_bitcast_fusion.5
  128.5 4.1 %multiply_convert_fusion.2 = bf16[8,128,18,128]{1,3,2,0:T(8,128)(2,1)S(1)} fusion(f32[8,128]{1,0:T(8,128)S(1)} %bitcast.192, bf16[128,8,64,1]{0,2,3,1:T(8,128)(2,1)S(1)} %bitcast.178, bf16[18,128,8,64]{1,3,2,0:T(8,128)(2,1)S(1)} %bitcast.170, f32[8,128]{1,0:T(8,128)S(1)} %fusion.99, f32[8,128]{1,0:T(8,128)S(1)} %get-tuple-element.221, ...), kind=kOutput, calls=%fused_computation.2.clone.1 | convolution fusion | flops 320864256 | bytes 16658450 | tf_op jit(solution)/shard_map/while/body/eval_jaxpr/ihd,kjhd->hikj/dot_general | solution.py:33
  132.6 1.1 fusion.102
  133.7 1.7 convolution_bitcast_fusion.6
  135.5 4.5 %copy_dynamic-update-slice_fusion.3 = (f32[2,18,128,8,64]{2,4,3,1,0:T(8,128)}, f32[2,18,128,8,64]{2,4,3,1,0:T(8,128)}) fusion(f32[2,18,128,8,64]{2,4,3,1,0:T(8,128)} %get-tuple-element.237, s32[]{:T(128)S(6)} %copy.268, f32[1,18,128,8,64]{2,4,1,3,0:T(8,128)S(1)} %convolution_bitcast_fusion.5, f32[2,18,128,8,64]{2,4,3,1,0:T(8,128)} %get-tuple-element.236, ...), kind=kLoop, calls=%fused_computation.8.clone.1 | loop fusion | bytes 18874372 | tf_op jit(solution)/shard_map/while/body/jit(dynamic_update_index_in_dim)/dynamic_update_slice | solution.py:108
  140.0 0.9 constant_dynamic-slice_fusion.12
  141.2 1.8 constant_dynamic-slice_fusion.10
  143.1 2.7 constant_dynamic-slice_fusion.9
  145.8 1.5 copy-done
  147.3 2.1 fusion.98
  149.4 1.9 fusion.99
  151.3 2.4 fusion.100
  153.7 1.1 fusion.101
  154.8 1.7 convolution_bitcast_fusion.5
  156.6 4.1 %multiply_convert_fusion.2 = bf16[8,128,18,128]{1,3,2,0:T(8,128)(2,1)S(1)} fusion(f32[8,128]{1,0:T(8,128)S(1)} %bitcast.192, bf16[128,8,64,1]{0,2,3,1:T(8,128)(2,1)S(1)} %bitcast.178, bf16[18,128,8,64]{1,3,2,0:T(8,128)(2,1)S(1)} %bitcast.170, f32[8,128]{1,0:T(8,128)S(1)} %fusion.99, f32[8,128]{1,0:T(8,128)S(1)} %get-tuple-element.221, ...), kind=kOutput, calls=%fused_computation.2.clone.1 | convolution fusion | flops 320864256 | bytes 16658450 | tf_op jit(solution)/shard_map/while/body/eval_jaxpr/ihd,kjhd->hikj/dot_general | solution.py:33
  160.7 1.1 fusion.102
  161.8 1.7 convolution_bitcast_fusion.6
  163.5 4.6 %copy_dynamic-update-slice_fusion.3 = (f32[2,18,128,8,64]{2,4,3,1,0:T(8,128)}, f32[2,18,128,8,64]{2,4,3,1,0:T(8,128)}) fusion(f32[2,18,128,8,64]{2,4,3,1,0:T(8,128)} %get-tuple-element.237, s32[]{:T(128)S(6)} %copy.268, f32[1,18,128,8,64]{2,4,1,3,0:T(8,128)S(1)} %convolution_bitcast_fusion.5, f32[2,18,128,8,64]{2,4,3,1,0:T(8,128)} %get-tuple-element.236, ...), kind=kLoop, calls=%fused_computation.8.clone.1 | loop fusion | bytes 18874372 | tf_op jit(solution)/shard_map/while/body/jit(dynamic_update_index_in_dim)/dynamic_update_slice | solution.py:108
  168.2 9.6 %copy.179 = f32[1,2,18,128,512]{4,3,0,2,1:T(8,128)} copy(f32[1,2,18,128,512]{3,4,2,1,0:T(8,128)} %bitcast.179) | data formatting | bytes 18874368 | tf_op jit(solution)/shard_map/stack;reshape | solution.py:119
  177.9 9.6 %copy.178 = f32[1,2,18,128,512]{4,3,0,2,1:T(8,128)} copy(f32[1,2,18,128,512]{3,4,2,1,0:T(8,128)} %bitcast.180) | data formatting | bytes 18874368 | tf_op jit(solution)/shard_map/stack;reshape | solution.py:119
  187.5 6.9 %pad_maximum_fusion = f32[2,2,16,128,512]{4,3,0,2,1:T(8,128)S(1)} fusion(f32[1,2,18,128,512]{4,3,0,2,1:T(8,128)} %copy.179, f32[1,2,18,128,512]{4,3,0,2,1:T(8,128)} %copy.178), kind=kLoop, calls=%fused_computation.31 | loop fusion | flops 4194304 | bytes 35651584 | tf_op jit(solution)/shard_map/stack | solution.py:119
  194.4 17.5 %copy.182 = f32[2,2,16,128,512]{4,2,1,3,0:T(8,128)S(1)} copy(f32[2,2,16,128,512]{4,3,0,2,1:T(8,128)S(1)} %pad_maximum_fusion) | data formatting | bytes 33554432 | tf_op jit(solution)/shard_map/slice | solution.py:135
  211.9 10.7 %convolution_bitcast_fusion.2 = f32[2,16,1,128,512]{4,1,3,0,2:T(8,128)S(1)} fusion(f32[2,32,128,512]{3,1,2,0:T(8,128)S(1)} %bitcast.168, s32[32]{0:T(128)S(1)} %copy-done.15, s32[32]{0:T(128)S(1)} %copy-done.13, pred[32]{0:T(512)(128)(4,1)S(1)} %copy-done.11), kind=kOutput, calls=%fused_computation.39 | convolution fusion | flops 805308416 | bytes 25166112 | tf_op jit(solution)/shard_map/es,xejw->xsjw/dot_general | solution.py:137
  222.5 8.1 %copy.183 = f32[2,16,1,128,512]{4,3,0,2,1:T(8,128)} copy(f32[2,16,1,128,512]{4,1,3,0,2:T(8,128)S(1)} %convolution_bitcast_fusion.2) | data formatting | bytes 16777216 | tf_op jit(solution)/shard_map/reshape | solution.py:138
  230.7 6.9 %all-to-all-start.2 = ((f32[2,16,1,128,512]{4,3,0,2,1:T(8,128)}), f32[2,16,1,128,512]{4,3,0,2,1:T(8,128)}, u32[]{:S(2)}, u32[]{:S(2)}) async-start(f32[2,16,1,128,512]{4,3,0,2,1:T(8,128)} %copy.183), calls=%async_computation.2 | async-start | bytes 16777216 | tf_op jit(solution)/shard_map/all_to_all | solution.py:139
  237.6 1.3 maximum_bitcast_fusion.1
  238.9 2.1 collective-permute-start.1
  241.4 1.0 reshape.387
  242.4 1.3 fusion.33
  243.7 3.8 %collective-permute-done.1 = f32[2,128,512]{2,1,0:T(8,128)S(1)} collective-permute-done((f32[2,128,512]{2,1,0:T(8,128)S(1)}, f32[2,128,512]{2,1,0:T(8,128)S(1)}, u32[]{:S(2)}, u32[]{:S(2)}) %collective-permute-start.1) | collective-permute-done | bytes 524320 | tf_op jit(solution)/shard_map/ppermute | solution.py:16
  247.5 0.4 broadcast_in_dim.48
  247.9 96.4 %all-to-all-done.2 = f32[2,16,1,128,512]{4,3,0,2,1:T(8,128)} async-done(((f32[2,16,1,128,512]{4,3,0,2,1:T(8,128)}), f32[2,16,1,128,512]{4,3,0,2,1:T(8,128)}, u32[]{:S(2)}, u32[]{:S(2)}) %all-to-all-start.2) | async-done | bytes 8388640 | tf_op jit(solution)/shard_map/all_to_all | solution.py:139
  344.2 11.9 %fusion.35 = bf16[2,2,128,512]{3,1,2,0:T(2,128)(2,1)S(1)} fusion(f32[2,2,128,512]{3,2,0,1:T(8,128)S(1)} %fusion.33, f32[2,1,128,512]{3,1,2,0:T(1,128)S(1)} %broadcast_in_dim.48, f32[2,16,1,128,512]{4,3,0,2,1:T(8,128)} %all-to-all-done.2, s32[16]{0:T(128)S(1)} %copy-done.16), kind=kOutput, calls=%fused_computation.45 | convolution fusion | flops 51118112 | bytes 10485824 | tf_op jit(solution)/shard_map/sb,xsjw->xbjw/dot_general | solution.py:143
  356.2 0.4 fusion.59
  356.5 0.7 copy.186
  357.3 0.7 copy.185
  (78 shorter events, 1.8 us)
Async XLA Ops:
  1.4 8.7 %copy-start.10 = (pred[32]{0:T(512)(128)(4,1)}, pred[32]{0:T(512)(128)(4,1)S(1)}, u32[]{:S(2)}) copy-start(pred[32]{0:T(512)(128)(4,1)S(1)} %broadcast_compare_fusion.1) | copy-start | bytes 100
  1.4 8.7 %copy-start.12 = (s32[32]{0:T(128)}, s32[32]{0:T(128)S(1)}, u32[]{:S(2)}) copy-start(s32[32]{0:T(128)S(1)} %get-tuple-element.159) | copy-start | bytes 388
  1.7 0.5 copy-start.14
  3.0 10.8 %all-to-all-start = ((s32[16,1,1]{2,1,0:T(1,128)}), s32[16,1,1]{2,1,0:T(1,128)S(1)}, u32[]{:S(2)}, u32[]{:S(2)}) async-start(s32[16,1,1]{2,1,0:T(1,128)} %copy.167), calls=%async_computation | async-start | bytes 16384 | tf_op jit(solution)/shard_map/all_to_all | solution.py:79
  14.8 11.1 %copy-start.4 = (bf16[256,512]{1,0:T(8,128)(2,1)S(1)}, bf16[256,512]{1,0:T(8,128)(2,1)}, u32[]{:S(2)}) copy-start(bf16[256,512]{1,0:T(8,128)(2,1)} %param.9) | copy-start | bytes 786436
  14.8 11.1 %copy-start.5 = (bf16[256,512]{1,0:T(8,128)(2,1)S(1)}, bf16[256,512]{1,0:T(8,128)(2,1)}, u32[]{:S(2)}) copy-start(bf16[256,512]{1,0:T(8,128)(2,1)} %param.8) | copy-start | bytes 786436
  14.8 13.0 %copy-start.17 = (s32[2,16]{1,0:T(2,128)S(1)}, s32[2,16]{1,0:T(2,128)}, u32[]{:S(2)}) copy-start(s32[2,16]{1,0:T(2,128)} %param.11) | copy-start | bytes 388
  17.7 60.6 %all-to-all-start.1 = ((bf16[2,16,1,128,512]{4,3,0,2,1:T(8,128)(2,1)}), bf16[2,16,1,128,512]{4,3,0,2,1:T(8,128)(2,1)}, u32[]{:S(2)}, u32[]{:S(2)}) async-start(bf16[2,16,1,128,512]{4,3,0,2,1:T(8,128)(2,1)} %bitcast.175), calls=%async_computation.1 | async-start | bytes 8388608 | tf_op jit(solution)/shard_map/all_to_all | solution.py:81
  25.9 7.7 %collective-permute-start = (bf16[2,128,512]{2,1,0:T(8,128)(2,1)S(1)}, bf16[2,128,512]{2,1,0:T(8,128)(2,1)S(1)}, u32[]{:S(2)}, u32[]{:S(2)}) collective-permute-start(bf16[2,128,512]{2,1,0:T(8,128)(2,1)S(1)} %pad_maximum_fusion.3), channel_id=1, source_target_pairs={{0,1},{1,2},{2,3},{3,4},{4,5},{5,6},{6,7},{8,9},{9,10},{10,11},{11... | collective-permute-start | bytes 786440 | tf_op jit(solution)/shard_map/ppermute | solution.py:16
  106.7 4.9 %copy-start.6 = (bf16[256,512]{1,0:T(8,128)(2,1)S(1)}, bf16[256,512]{1,0:T(8,128)(2,1)}, u32[]{:S(2)}) copy-start(bf16[256,512]{1,0:T(8,128)(2,1)} %param.7) | copy-start | bytes 786436
  115.0 10.6 %copy-start.2 = (bf16[1,18,128,512]{2,3,1,0:T(8,128)(2,1)}, bf16[1,18,128,512]{2,3,1,0:T(8,128)(2,1)S(1)}, u32[]{:S(2)}) copy-start(bf16[1,18,128,512]{2,3,1,0:T(8,128)(2,1)S(1)} %constant_dynamic-slice_fusion.10) | copy-start | bytes 7077892 | tf_op jit(solution)/shard_map/while
  117.7 1.5 copy-start
  126.7 1.8 copy-start.3
  128.5 4.1 %copy-start.1 = (bf16[1,18,128,512]{2,3,1,0:T(8,128)(2,1)S(1)}, bf16[1,18,128,512]{2,3,1,0:T(8,128)(2,1)}, u32[]{:S(2)}) copy-start(bf16[1,18,128,512]{2,3,1,0:T(8,128)(2,1)} %copy-done) | copy-start | bytes 7077892 | tf_op jit(solution)/shard_map/while
  128.5 4.1 %copy-start.7 = (bf16[2,128,8,64]{1,3,2,0:T(8,128)(2,1)S(1)}, bf16[2,128,8,64]{1,3,2,0:T(8,128)(2,1)}, u32[]{:S(2)}) copy-start(bf16[2,128,8,64]{1,3,2,0:T(8,128)(2,1)} %get-tuple-element.235) | copy-start | bytes 786436 | tf_op jit(solution)/shard_map/while
  133.7 6.3 %copy-start.8 = (bf16[2,128,8,64]{1,3,2,0:T(8,128)(2,1)}, bf16[2,128,8,64]{1,3,2,0:T(8,128)(2,1)S(1)}, u32[]{:S(2)}) copy-start(bf16[2,128,8,64]{1,3,2,0:T(8,128)(2,1)S(1)} %fusion.102) | copy-start | bytes 786436 | tf_op jit(solution)/shard_map/while
  143.1 10.6 %copy-start.2 = (bf16[1,18,128,512]{2,3,1,0:T(8,128)(2,1)}, bf16[1,18,128,512]{2,3,1,0:T(8,128)(2,1)S(1)}, u32[]{:S(2)}) copy-start(bf16[1,18,128,512]{2,3,1,0:T(8,128)(2,1)S(1)} %constant_dynamic-slice_fusion.10) | copy-start | bytes 7077892 | tf_op jit(solution)/shard_map/while
  145.7 1.5 copy-start
  154.8 1.8 copy-start.3
  156.5 4.1 %copy-start.1 = (bf16[1,18,128,512]{2,3,1,0:T(8,128)(2,1)S(1)}, bf16[1,18,128,512]{2,3,1,0:T(8,128)(2,1)}, u32[]{:S(2)}) copy-start(bf16[1,18,128,512]{2,3,1,0:T(8,128)(2,1)} %copy-done) | copy-start | bytes 7077892 | tf_op jit(solution)/shard_map/while
  156.6 4.1 %copy-start.7 = (bf16[2,128,8,64]{1,3,2,0:T(8,128)(2,1)S(1)}, bf16[2,128,8,64]{1,3,2,0:T(8,128)(2,1)}, u32[]{:S(2)}) copy-start(bf16[2,128,8,64]{1,3,2,0:T(8,128)(2,1)} %get-tuple-element.235) | copy-start | bytes 786436 | tf_op jit(solution)/shard_map/while
  161.7 6.3 %copy-start.8 = (bf16[2,128,8,64]{1,3,2,0:T(8,128)(2,1)}, bf16[2,128,8,64]{1,3,2,0:T(8,128)(2,1)S(1)}, u32[]{:S(2)}) copy-start(bf16[2,128,8,64]{1,3,2,0:T(8,128)(2,1)S(1)} %fusion.102) | copy-start | bytes 786436 | tf_op jit(solution)/shard_map/while
  194.3 17.5 %copy-start.11 = (pred[32]{0:T(512)(128)(4,1)S(1)}, pred[32]{0:T(512)(128)(4,1)}, u32[]{:S(2)}) copy-start(pred[32]{0:T(512)(128)(4,1)} %copy-done.10) | copy-start | bytes 100
  194.3 17.5 %copy-start.13 = (s32[32]{0:T(128)S(1)}, s32[32]{0:T(128)}, u32[]{:S(2)}) copy-start(s32[32]{0:T(128)} %copy-done.12) | copy-start | bytes 388
  194.3 17.5 %copy-start.15 = (s32[32]{0:T(128)S(1)}, s32[32]{0:T(128)}, u32[]{:S(2)}) copy-start(s32[32]{0:T(128)} %copy-done.14) | copy-start | bytes 388
  230.7 113.6 %all-to-all-start.2 = ((f32[2,16,1,128,512]{4,3,0,2,1:T(8,128)}), f32[2,16,1,128,512]{4,3,0,2,1:T(8,128)}, u32[]{:S(2)}, u32[]{:S(2)}) async-start(f32[2,16,1,128,512]{4,3,0,2,1:T(8,128)} %copy.183), calls=%async_computation.2 | async-start | bytes 16777216 | tf_op jit(solution)/shard_map/all_to_all | solution.py:139
  237.6 3.5 copy-start.9
  238.9 8.6 %collective-permute-start.1 = (f32[2,128,512]{2,1,0:T(8,128)S(1)}, f32[2,128,512]{2,1,0:T(8,128)S(1)}, u32[]{:S(2)}, u32[]{:S(2)}) collective-permute-start(f32[2,128,512]{2,1,0:T(8,128)S(1)} %get-tuple-element.151), channel_id=1, source_target_pairs={{1,0},{2,1},{3,2},{4,3},{5,4},{6,5},{7,6},{9,8},{10,9},{11,10},{12... | collective-permute-start | bytes 1572872 | tf_op jit(solution)/shard_map/ppermute | solution.py:16
  242.4 101.8 %copy-start.16 = (s32[16]{0:T(128)S(1)}, s32[16]{0:T(128)}, u32[]{:S(2)}) copy-start(s32[16]{0:T(128)} %get-tuple-element.127) | copy-start | bytes 196
where the time goes:
time: 363 us; the launch traced here: 358 us
  waiting for transfers between devices  151 us (42%)
  local copies, waits for them, and re-layouts  107 us (29%)
  matrix products  46.2 us (13%)
  starting transfers between devices  26.3 us (7%)
  other arithmetic  25.9 us (7%)
    all_to_all x1, waiting for transfers between devices, shards(): lax.all_to_all(outgoing, 'views', split_axis=1, concat_axis=1, tiled=True)  96.4 us
    all_to_all x1, waiting for transfers between devices, shards(): lax.all_to_all(offered, 'views', split_axis=1, concat_axis=1, tiled=True)  42.6 us
    another operation x2, local copies, waits for them, and re-layouts, shards(): jnp.stack([key_part.reshape(block_count, set_size, block_rows, feature_wi...  19.2 us
    slice x1, local copies, waits for them, and re-layouts, shards(): gradients[:, :, 2:].reshape(2, entry_count, block_rows, feature_width)  17.5 us
    dot_general x1, matrix products, shards(): jnp.einsum('sb,xsjw->xbjw', owner_match, arrived.reshape(2, view_count *...  11.9 us
    reshape x1, local copies, waits for them, and re-layouts, shards(): picked.reshape(2, block_count, list_slots, block_rows, feature_width)  11.4 us
    dynamic_slice x12, local copies, waits for them, and re-layouts, shards(): lax.map(per_block, (queries.reshape(block_count, block_rows, feature_widt...  11.3 us
    dot_general x1, matrix products, shards(): jnp.einsum('es,xejw->xsjw', chooser, entry_grads, precision=lax.Precision...  10.7 us
  transfers between devices with their start and end apart: 5, of which 5 were waited for; matrix products, arithmetic and copies ran while one was open for 2% of the time, Pallas kernels for 0%

commit v1 on v0

v1 whole, which is shorter than its diff:
```python
import jax
import jax.numpy as jnp
from jax import lax
from jax.experimental import pallas as pl
from jax.experimental.pallas import tpu as pltpu
from jax.sharding import PartitionSpec as P

MESH = pl.DeviceIdType.MESH
F32 = jnp.float32
BF16 = jnp.bfloat16
SIDE = 4
BLK = 128
WIDTH = 512
HALF = 256
PAIRS = 4
LOCAL = 16
ENTRIES = 19
FAR = 1e30


def nt(a, b):
    return lax.dot_general(a, b, (((1,), (1,)), ((), ())), preferred_element_type=F32)


def nn(a, b):
    return lax.dot_general(a, b, (((1,), (0,)), ((), ())), preferred_element_type=F32)


def tn(a, b):
    return lax.dot_general(a, b, (((0,), (0,)), ((), ())), preferred_element_type=F32)


def pick(first, second, second_weight):
    return first * (1 - second_weight) + second * second_weight


def kernel(
    lists_ref,
    q_ref,
    k_ref,
    v_ref,
    g_ref,
    dq_ref,
    dk_ref,
    dv_ref,
    qs_ref,
    meta_ref,
    meta_x,
    meta_y,
    near,
    stage,
    kv_in,
    qg_in,
    raised_buf,
    grad_buf,
    max_buf,
    sum_buf,
    scale_buf,
    delta_buf,
    stat_out,
    stat_in,
    dq_acc,
    dk_acc,
    dv_acc,
    meta_ss,
    meta_rs,
    near_ss,
    near_rs,
    far_ss,
    far_rs,
    win_ss,
    win_rs,
    stat_ss,
    stat_rs,
):
    me = lax.axis_index("views")
    band = lax.axis_index("sub")
    bands = lax.axis_size("sub")
    x, y = me // SIDE, me % SIDE
    after = lax.rem(band + 1, bands)
    ahead = lax.rem(band + bands - 1, bands)

    def view(a, b):
        return lax.rem(x + (a % SIDE), SIDE) * SIDE + lax.rem(y + (b % SIDE), SIDE)

    offsets = [(a, b) for a in range(SIDE) for b in range(SIDE) if (a, b) != (0, 0)]

    barrier = pltpu.get_barrier_semaphore()
    for a, b in offsets:
        pl.semaphore_signal(
            barrier, inc=1, device_id={"views": view(a, b)}, device_id_type=MESH
        )
    for s in (after, ahead):
        pl.semaphore_signal(barrier, inc=1, device_id={"sub": s}, device_id_type=MESH)

    lists = lists_ref[...]
    views = lax.broadcasted_iota(jnp.int32, (16, 16), 0)
    found = []
    for row in range(2):
        ids = jnp.broadcast_to(lists[row : row + 1, :], (16, 16))
        hit = (ids >= 0) & ((ids >> 4) == views)
        live = jnp.sum(jnp.where(hit, 1.0, 0.0), axis=1, keepdims=True)
        odd = jnp.sum(jnp.where(hit & ((ids & 1) == 1), 1.0, 0.0), axis=1, keepdims=True)
        found.append((live, odd))
    meta_ref[0] = jnp.broadcast_to(found[0][1] + found[1][1], (16, 128))
    meta_ref[1] = jnp.broadcast_to(found[1][0], (16, 128))
    meta_ref[2] = jnp.broadcast_to(found[0][0] + found[1][0], (16, 128))
    qs_ref[...] = q_ref[...] * jnp.asarray(0.125, BF16)

    pl.semaphore_wait(barrier, 17)

    sent = []

    def copy(src, dst, ss, rs, **to):
        c = pltpu.make_async_remote_copy(
            src_ref=src,
            dst_ref=dst,
            send_sem=ss,
            recv_sem=rs,
            device_id=to,
            device_id_type=MESH,
        )
        c.start()
        sent.append(c)
        return c

    metas = {}
    for d in (1, 3, 2):
        metas["x", d] = copy(
            meta_ref.at[0:2],
            meta_x.at[d - 1],
            meta_ss.at[0, d - 1],
            meta_rs.at[0, d - 1],
            views=view(-d, 0),
        )
        metas["y", d] = copy(
            meta_ref.at[0:2],
            meta_y.at[d - 1],
            meta_ss.at[1, d - 1],
            meta_rs.at[1, d - 1],
            views=view(0, -d),
        )

    own = ((k_ref, v_ref), (qs_ref, g_ref))
    nears = {}

    def send_near(group):
        for d in (1, 3, 2):
            for arr in range(2):
                for half in range(2):
                    nears[group, half, d, arr] = copy(
                        own[group][arr].at[:, half * HALF : (half + 1) * HALF],
                        near.at[group, half, d - 1, arr],
                        near_ss.at[group, half, d - 1, arr],
                        near_rs.at[group, half, d - 1, arr],
                        views=view(d, 0) if half == 0 else view(0, d),
                    )

    wins = {}

    def send_window(group):
        rows = slice(BLK, 2 * BLK) if group == 0 else slice(0, BLK)
        target = kv_in if group == 0 else qg_in
        for arr in range(2):
            for half in range(2):
                wins[group, half, arr] = copy(
                    own[group][arr].at[rows, half * HALF : (half + 1) * HALF],
                    target.at[0, half, arr],
                    win_ss.at[group, half, arr],
                    win_rs.at[group, half, arr],
                    sub=after if group == 0 else ahead,
                )

    send_near(0)
    send_window(0)
    send_window(1)
    send_near(1)

    lane = lax.broadcasted_iota(jnp.int32, (1, 128), 1)
    low = jnp.where(lane < 64, 1.0, 0.0)
    low16, high16 = low.astype(BF16), (1.0 - low).astype(BF16)

    def stack(piece):
        return jnp.concatenate([piece * low16, piece * high16], axis=0)

    def wide(row):
        return jnp.concatenate([row, row], axis=1)

    def forward(entry, p, qp, gp, kp, vp):
        scores = nt(kp, stack(qp))
        grads = nt(vp, stack(gp))
        top = jnp.max(scores, axis=0, keepdims=True)
        raised = jnp.exp(scores - top)
        raised_buf[entry, p] = raised
        grad_buf[entry, p] = grads
        max_buf[entry, p : p + 1, :] = top
        sum_buf[entry, p : p + 1, :] = jnp.sum(raised, axis=0, keepdims=True)

    def local_forward(n, carry):
        q_rows = pl.ds(pl.multiple_of(jnp.minimum(n, 1) * BLK, BLK), BLK)
        k_rows = pl.ds(pl.multiple_of((n // 2) * BLK, BLK), BLK)
        for p in range(PAIRS):
            cols = slice(p * 128, (p + 1) * 128)
            forward(
                LOCAL + n,
                p,
                qs_ref[q_rows, cols],
                g_ref[q_rows, cols],
                k_ref[k_rows, cols],
                v_ref[k_rows, cols],
            )
        return carry

    lax.fori_loop(0, 3, local_forward, 0)

    for c in metas.values():
        c.wait_recv()

    def meta_of(axis, d, plane, row):
        if d % SIDE == 0:
            got = meta_ref[plane, pl.ds(row, 1), :]
        elif axis == "x":
            got = meta_x[d % SIDE - 1, plane, pl.ds(row, 1), :]
        else:
            got = meta_y[d % SIDE - 1, plane, pl.ds(row, 1), :]
        return got.astype(BF16)

    def want(group, half, j, d):
        if group == 0 and half == 0:
            return meta_of("y", d, 0, view(-j, 0))
        if group == 0:
            return meta_of("x", d, 0, view(0, -j))
        if half == 0:
            return meta_of("x", -j, 1, view(0, d))
        return meta_of("y", -j, 1, view(d, 0))

    fars = {}

    def send_far(group, j):
        for half in range(2):
            if j:
                for arr in range(2):
                    nears[group, half, j, arr].wait_recv()
            target = kv_in if group == 0 else qg_in
            for d in (1, 3, 2, 0):
                if d == 0 and j == 0:
                    continue
                slot = j * SIDE + d if half == 0 else d * SIDE + j
                weight = want(group, half, j, d)
                weight = wide(weight)
                for arr in range(2):
                    if j:
                        first = near[group, half, j - 1, arr, 0:BLK, :]
                        second = near[group, half, j - 1, arr, BLK : 2 * BLK, :]
                    else:
                        cols = slice(half * HALF, (half + 1) * HALF)
                        first = own[group][arr][0:BLK, cols]
                        second = own[group][arr][BLK : 2 * BLK, cols]
                    chosen = pick(first, second, weight)
                    if d:
                        stage[group, half, j, d - 1, arr] = chosen
                    else:
                        target[slot, half, arr] = chosen
                if d:
                    fars[group, half, slot] = copy(
                        stage.at[group, half, j, d - 1],
                        target.at[slot, half],
                        far_ss.at[group, half, j, d - 1],
                        far_rs.at[group, half, j, d - 1],
                        views=view(0, d) if half == 0 else view(d, 0),
                    )

    for j in (0, 1, 3, 2):
        send_far(0, j)
    for j in (0, 1, 3, 2):
        send_far(1, j)

    def view_of_slot(i):
        return lax.rem(x + SIDE - i // SIDE, SIDE) * SIDE + lax.rem(y + SIDE - i % SIDE, SIDE)

    def remote_forward(i, carry):
        weight = meta_ref[1, pl.ds(view_of_slot(i), 1), :].astype(BF16)
        for p in range(PAIRS):
            cols = slice(p * 128, (p + 1) * 128)
            inner = slice((p % 2) * 128, (p % 2 + 1) * 128)
            forward(
                i,
                p,
                pick(qs_ref[0:BLK, cols], qs_ref[BLK : 2 * BLK, cols], weight),
                pick(g_ref[0:BLK, cols], g_ref[BLK : 2 * BLK, cols], weight),
                kv_in[i, p // 2, 0, :, inner],
                kv_in[i, p // 2, 1, :, inner],
            )
        return carry

    for c in (wins[0, h, r] for h in range(2) for r in range(2)):
        c.wait_recv()
    for a in (0, 1, 3, 2):
        for b in range(SIDE):
            slot = a * SIDE + b
            for half in range(2):
                if (0, half, slot) in fars:
                    fars[0, half, slot].wait_recv()
        lax.fori_loop(a * SIDE, (a + 1) * SIDE, remote_forward, 0)

    has_prev = jnp.where(band > 0, 1.0, 0.0)
    ones = jnp.full((1, HALF), 1.0, F32)
    uses = []
    for e in range(ENTRIES):
        if e == 0:
            uses.append((ones * has_prev, ones * 0.0))
        elif e < LOCAL:
            row = view(-(e // SIDE), -(e % SIDE))
            second = wide(meta_ref[1, pl.ds(row, 1), :])
            live = wide(meta_ref[2, pl.ds(row, 1), :])
            uses.append((live * (1.0 - second), live * second))
        else:
            second = ones * (0.0 if e == LOCAL else 1.0)
            uses.append((1.0 - second, second))
    tops, invs = [], []
    for blk in range(2):
        top = jnp.full((PAIRS, HALF), -FAR, F32)
        for e in range(ENTRIES):
            top = jnp.maximum(top, max_buf[e] + (uses[e][blk] - 1.0) * FAR)
        tops.append(top)
        total = jnp.zeros((PAIRS, HALF), F32)
        for e in range(ENTRIES):
            total += uses[e][blk] * sum_buf[e] * jnp.exp(jnp.minimum(max_buf[e] - top, 0.0))
        invs.append(1.0 / total)
    for e in range(ENTRIES):
        scale_buf[e] = sum(
            uses[e][blk] * jnp.exp(jnp.minimum(max_buf[e] - tops[blk], 0.0)) * invs[blk]
            for blk in range(2)
        )

    def delta_part(e, carry):
        for p in range(PAIRS):
            prob = raised_buf[e, p] * scale_buf[e, p : p + 1, :]
            rounded = prob.astype(BF16).astype(F32)
            delta_buf[e, p : p + 1, :] = jnp.sum(rounded * grad_buf[e, p], axis=0, keepdims=True)
        return carry

    lax.fori_loop(0, ENTRIES, delta_part, 0)
    deltas = [
        sum(uses[e][blk] * delta_buf[e] for e in range(ENTRIES)) for blk in range(2)
    ]
    stats = {}
    for e in range(ENTRIES):
        first, second = uses[e]
        delta = first * deltas[0] + second * deltas[1]
        delta_buf[e] = delta
        if e < LOCAL:
            a, b = e // SIDE, e % SIDE
            stat_out[e, 0:4, :] = (
                first * tops[0] + second * tops[1] + (1.0 - first - second) * FAR
            )
            stat_out[e, 4:8, :] = first * invs[0] + second * invs[1]
            stat_out[e, 8:12, :] = delta
            if e:
                stat_out[e, 12:16, :] = jnp.broadcast_to(
                    wide(meta_ref[0, pl.ds(view(-a, -b), 1), :]), (4, HALF)
                )
            else:
                stat_out[e, 12:16, :] = jnp.ones((4, HALF), F32)
            slot = (-a % SIDE) * SIDE + (-b % SIDE)
            to = {"views": view(-a, -b)} if e else {"sub": ahead}
            stats[slot] = copy(
                stat_out.at[e], stat_in.at[slot], stat_ss.at[slot], stat_rs.at[slot], **to
            )

    dq_acc[...] = jnp.zeros_like(dq_acc)
    dk_acc[...] = jnp.zeros_like(dk_acc)
    dv_acc[...] = jnp.zeros_like(dv_acc)

    def score_gradient(e, p):
        prob = raised_buf[e, p] * scale_buf[e, p : p + 1, :]
        return prob, (prob * (grad_buf[e, p] - delta_buf[e, p : p + 1, :])).astype(BF16)

    def halves(both):
        return jnp.where(lane < 64, both[0:BLK, :], both[BLK : 2 * BLK, :])

    def local_backward(n, carry):
        q_rows = pl.ds(pl.multiple_of(jnp.minimum(n, 1) * BLK, BLK), BLK)
        k_rows = pl.ds(pl.multiple_of((n // 2) * BLK, BLK), BLK)
        for p in range(PAIRS):
            cols = slice(p * 128, (p + 1) * 128)
            prob, ds = score_gradient(LOCAL + n, p)
            dq_acc[q_rows, cols] += halves(tn(ds, k_ref[k_rows, cols]))
            dk_acc[k_rows, cols] += nn(ds, stack(qs_ref[q_rows, cols]))
            dv_acc[k_rows, cols] += nn(prob.astype(BF16), stack(g_ref[q_rows, cols]))
        return carry

    lax.fori_loop(0, 3, local_backward, 0)

    def remote_backward(i, carry):
        weight = meta_ref[1, pl.ds(view_of_slot(i), 1), :]
        weight = jnp.where(i == 0, 0.0, weight)
        for p in range(PAIRS):
            cols = slice(p * 128, (p + 1) * 128)
            inner = slice((p % 2) * 128, (p % 2 + 1) * 128)
            _, ds = score_gradient(i, p)
            part = halves(tn(ds, kv_in[i, p // 2, 0, :, inner]))
            dq_acc[0:BLK, cols] += part * (1.0 - weight)
            dq_acc[BLK : 2 * BLK, cols] += part * weight
        return carry

    lax.fori_loop(0, LOCAL, remote_backward, 0)
    dq_ref[...] = (dq_acc[...] * 0.125).astype(BF16)

    def owner_backward(i, carry):
        weight = stat_in[i, 12:13, 0:128]
        weight16 = weight.astype(BF16)
        for p in range(PAIRS):
            cols = slice(p * 128, (p + 1) * 128)
            inner = slice((p % 2) * 128, (p % 2 + 1) * 128)
            kp = pick(k_ref[0:BLK, cols], k_ref[BLK : 2 * BLK, cols], weight16)
            vp = pick(v_ref[0:BLK, cols], v_ref[BLK : 2 * BLK, cols], weight16)
            qp = stack(qg_in[i, p // 2, 0, :, inner])
            gp = stack(qg_in[i, p // 2, 1, :, inner])
            prob = jnp.exp(nt(kp, qp) - stat_in[i, p : p + 1, :]) * stat_in[i, 4 + p : 5 + p, :]
            ds = (prob * (nt(vp, gp) - stat_in[i, 8 + p : 9 + p, :])).astype(BF16)
            dk = nn(ds, qp)
            dv = nn(prob.astype(BF16), gp)
            dk_acc[0:BLK, cols] += dk * (1.0 - weight)
            dk_acc[BLK : 2 * BLK, cols] += dk * weight
            dv_acc[0:BLK, cols] += dv * (1.0 - weight)
            dv_acc[BLK : 2 * BLK, cols] += dv * weight
        return carry

    for c in (wins[1, h, r] for h in range(2) for r in range(2)):
        c.wait_recv()
    for a in (0, 1, 3, 2):
        for b in range(SIDE):
            slot = a * SIDE + b
            stats[slot].wait_recv()
            for half in range(2):
                if (1, half, slot) in fars:
                    fars[1, half, slot].wait_recv()
        lax.fori_loop(a * SIDE, (a + 1) * SIDE, owner_backward, 0)

    dk_ref[...] = dk_acc[...].astype(BF16)
    dv_ref[...] = dv_acc[...].astype(BF16)
    for c in sent:
        c.wait_send()


def shards(queries, keys, values, out_grad, block_lists):
    vmem = pl.BlockSpec(memory_space=pltpu.VMEM)
    rows = 2 * BLK
    dma = pltpu.SemaphoreType.DMA
    stat_rows = (ENTRIES, PAIRS, HALF)
    return pl.pallas_call(
        kernel,
        out_shape=[jax.ShapeDtypeStruct((rows, WIDTH), BF16)] * 3,
        in_specs=[vmem] * 5,
        out_specs=[vmem] * 3,
        scratch_shapes=[
            pltpu.VMEM((rows, WIDTH), BF16),
            pltpu.VMEM((3, 16, 128), F32),
            pltpu.VMEM((3, 2, 16, 128), F32),
            pltpu.VMEM((3, 2, 16, 128), F32),
            pltpu.VMEM((2, 2, 3, 2, rows, HALF), BF16),
            pltpu.VMEM((2, 2, 4, 3, 2, BLK, HALF), BF16),
            pltpu.VMEM((16, 2, 2, BLK, HALF), BF16),
            pltpu.VMEM((16, 2, 2, BLK, HALF), BF16),
            pltpu.VMEM((ENTRIES, PAIRS, BLK, HALF), F32),
            pltpu.VMEM((ENTRIES, PAIRS, BLK, HALF), F32),
            pltpu.VMEM(stat_rows, F32),
            pltpu.VMEM(stat_rows, F32),
            pltpu.VMEM(stat_rows, F32),
            pltpu.VMEM(stat_rows, F32),
            pltpu.VMEM((16, 16, HALF), F32),
            pltpu.VMEM((16, 16, HALF), F32),
            pltpu.VMEM((rows, WIDTH), F32),
            pltpu.VMEM((rows, WIDTH), F32),
            pltpu.VMEM((rows, WIDTH), F32),
            dma((2, 3)),
            dma((2, 3)),
            dma((2, 2, 3, 2)),
            dma((2, 2, 3, 2)),
            dma((2, 2, 4, 3)),
            dma((2, 2, 4, 3)),
            dma((2, 2, 2)),
            dma((2, 2, 2)),
            dma((16,)),
            dma((16,)),
        ],
        compiler_params=pltpu.CompilerParams(
            collective_id=0, has_side_effects=True, vmem_limit_bytes=60 * 1024 * 1024
        ),
    )(block_lists, queries, keys, values, out_grad)


def solution(mesh):
    spec = P(("views", "sub"), None)
    return jax.shard_map(
        shards,
        mesh=mesh,
        in_specs=(spec,) * 5,
        out_specs=(spec,) * 3,
        check_vma=False,
    )
```

time: 363 us -> 100 us (0.28)
  the two profiles are of different devices: /device:TPU:92 before, /device:TPU:0 now
where the time goes in v1:
time: 100 us; the launch traced here: 99.9 us
  Pallas kernels  95.8 us (96%)
  local copies, waits for them, and re-layouts  3.46 us (3%)
    pallas_call x1, Pallas kernels, shards(): pl.pallas_call(kernel, out_shape=[jax.ShapeDtypeStruct((rows, WIDTH), BF1...  95.8 us
    unnamed x7, local copies, waits for them, and re-layouts  3.46 us

profile of v1, /device:TPU:0, one launch (start us, length us, event | category | flops | bytes accessed | tf_op | source)
XLA Modules:
  0.0 99.9 jit_solution(17260480998417948638)
XLA Ops:
  0.6 95.8 %shard_map.76 = (bf16[256,512]{1,0:T(8,128)(2,1)}, bf16[256,512]{1,0:T(8,128)(2,1)}, bf16[256,512]{1,0:T(8,128)(2,1)}) custom-call(s32[2,16]{1,0:T(2,128)} %lists_ref.1, bf16[256,512]{1,0:T(8,128)(2,1)} %q_ref.1, bf16[256,512]{1,0:T(8,128)(2,1)} %k_ref.1, bf16[256,512]{1,0:T(8,128)(2,1)} %v_ref.1, bf16[256,512]{1,0:T(8,128)(2,1)} %g_ref.1), custom_call_target="tpu_custom_call" | custom-call | tf_op jit(solution)/shard_map/pallas_call | solution.py:452
  96.5 0.0 copy-start.1
  96.5 1.7 %copy.11 = bf16[256,512]{1,0:T(8,128)(2,1)} copy(bf16[256,512]{1,0:T(8,128)(2,1)} %get-tuple-element.6) | data formatting | bytes 524288
  98.2 0.0 copy-done.1
  98.2 0.0 copy-start
  98.2 0.7 copy.12
  98.9 0.3 copy-done
  99.2 0.7 copy.13
Async XLA Ops:
  96.5 1.7 %copy-start.1 = (bf16[256,512]{1,0:T(8,128)(2,1)S(1)}, bf16[256,512]{1,0:T(8,128)(2,1)}, u32[]{:S(2)}) copy-start(bf16[256,512]{1,0:T(8,128)(2,1)} %get-tuple-element.7) | copy-start | bytes 786436
  98.2 1.0 %copy-start = (bf16[256,512]{1,0:T(8,128)(2,1)S(1)}, bf16[256,512]{1,0:T(8,128)(2,1)}, u32[]{:S(2)}) copy-start(bf16[256,512]{1,0:T(8,128)(2,1)} %get-tuple-element.8) | copy-start | bytes 786436

commit v2 on v1

--- a/solution.py
+++ b/solution.py
@@ -1,3 +1,5 @@
+import functools
+
 import jax
 import jax.numpy as jnp
 from jax import lax
@@ -145,14 +147,30 @@
     nears = {}
 
     def send_near(group):
-        for d in (1, 3, 2):
-            for arr in range(2):
+        for arr in range(2):
+            for d in (1, 3):
                 for half in range(2):
                     nears[group, half, d, arr] = copy(
                         own[group][arr].at[:, half * HALF : (half + 1) * HALF],
                         near.at[group, half, d - 1, arr],
                         near_ss.at[group, half, d - 1, arr],
                         near_rs.at[group, half, d - 1, arr],
+                        views=view(d, 0) if half == 0 else view(0, d),
+                    )
+
+    passed = {}
+
+    def pass_on(group):
+        for arr in range(2):
+            for d in (1, 3):
+                for half in range(2):
+                    nears[group, half, d, arr].wait_recv()
+                    rows = slice(0, BLK) if d == 1 else slice(BLK, 2 * BLK)
+                    passed[group, half, d, arr] = copy(
+                        near.at[group, half, d - 1, arr, rows, :],
+                        near.at[group, half, 1, arr, rows, :],
+                        near_ss.at[group, half, d, arr],
+                        near_rs.at[group, half, d, arr],
                         views=view(d, 0) if half == 0 else view(0, d),
                     )
 
@@ -174,7 +192,6 @@
     send_near(0)
     send_window(0)
     send_window(1)
-    send_near(1)
 
     lane = lax.broadcasted_iota(jnp.int32, (1, 128), 1)
     low = jnp.where(lane < 64, 1.0, 0.0)
@@ -237,17 +254,16 @@
     fars = {}
 
     def send_far(group, j):
-        for half in range(2):
-            if j:
-                for arr in range(2):
-                    nears[group, half, j, arr].wait_recv()
-            target = kv_in if group == 0 else qg_in
-            for d in (1, 3, 2, 0):
+        if j == 2:
+            for c in (passed[group, h, d, r] for h in range(2) for d in (1, 3) for r in range(2)):
+                c.wait_recv()
+        target = kv_in if group == 0 else qg_in
+        for d in (1, 3, 2, 0):
+            for half in range(2):
                 if d == 0 and j == 0:
                     continue
                 slot = j * SIDE + d if half == 0 else d * SIDE + j
-                weight = want(group, half, j, d)
-                weight = wide(weight)
+                weight = wide(want(group, half, j, d))
                 for arr in range(2):
                     if j:
                         first = near[group, half, j - 1, arr, 0:BLK, :]
@@ -270,17 +286,24 @@
                         views=view(0, d) if half == 0 else view(d, 0),
                     )
 
-    for j in (0, 1, 3, 2):
-        send_far(0, j)
-    for j in (0, 1, 3, 2):
-        send_far(1, j)
+    send_far(0, 0)
+    pass_on(0)
+    send_far(0, 1)
+    send_far(0, 3)
+    send_far(0, 2)
+    send_near(1)
 
     def view_of_slot(i):
         return lax.rem(x + SIDE - i // SIDE, SIDE) * SIDE + lax.rem(y + SIDE - i % SIDE, SIDE)
 
-    def remote_forward(i, carry):
+    def slot_of(half, j, n):
+        return j * SIDE + n if half == 0 else n * SIDE + j
+
+    def remote_forward(half, j, n, carry):
+        i = slot_of(half, j, n)
         weight = meta_ref[1, pl.ds(view_of_slot(i), 1), :].astype(BF16)
-        for p in range(PAIRS):
+        weight = weight * jnp.where(i == 0, 0.0, 1.0).astype(BF16)
+        for p in (2 * half, 2 * half + 1):
             cols = slice(p * 128, (p + 1) * 128)
             inner = slice((p % 2) * 128, (p % 2 + 1) * 128)
             forward(
@@ -288,20 +311,24 @@
                 p,
                 pick(qs_ref[0:BLK, cols], qs_ref[BLK : 2 * BLK, cols], weight),
                 pick(g_ref[0:BLK, cols], g_ref[BLK : 2 * BLK, cols], weight),
-                kv_in[i, p // 2, 0, :, inner],
-                kv_in[i, p // 2, 1, :, inner],
+                kv_in[i, half, 0, :, inner],
+                kv_in[i, half, 1, :, inner],
             )
         return carry
 
-    for c in (wins[0, h, r] for h in range(2) for r in range(2)):
-        c.wait_recv()
-    for a in (0, 1, 3, 2):
-        for b in range(SIDE):
-            slot = a * SIDE + b
-            for half in range(2):
-                if (0, half, slot) in fars:
-                    fars[0, half, slot].wait_recv()
-        lax.fori_loop(a * SIDE, (a + 1) * SIDE, remote_forward, 0)
+    def wait_items(group, half, j):
+        if j == 0:
+            for arr in range(2):
+                wins[group, half, arr].wait_recv()
+        for n in range(1, SIDE):
+            fars[group, half, slot_of(half, j, n)].wait_recv()
+
+    for j in (0, 1, 3, 2):
+        for half in range(2):
+            wait_items(0, half, j)
+            lax.fori_loop(0, SIDE, functools.partial(remote_forward, half, j), 0, unroll=4)
+        if j == 1:
+            send_far(1, 0)
 
     has_prev = jnp.where(band > 0, 1.0, 0.0)
     ones = jnp.full((1, HALF), 1.0, F32)
@@ -368,6 +395,10 @@
                 stat_out.at[e], stat_in.at[slot], stat_ss.at[slot], stat_rs.at[slot], **to
             )
 
+    pass_on(1)
+    send_far(1, 1)
+    send_far(1, 3)
+
     dq_acc[...] = jnp.zeros_like(dq_acc)
     dk_acc[...] = jnp.zeros_like(dk_acc)
     dv_acc[...] = jnp.zeros_like(dv_acc)
@@ -404,19 +435,21 @@
             dq_acc[BLK : 2 * BLK, cols] += part * weight
         return carry
 
-    lax.fori_loop(0, LOCAL, remote_backward, 0)
+    send_far(1, 2)
+    lax.fori_loop(0, LOCAL, remote_backward, 0, unroll=2)
     dq_ref[...] = (dq_acc[...] * 0.125).astype(BF16)
 
-    def owner_backward(i, carry):
+    def owner_backward(half, j, n, carry):
+        i = slot_of(half, j, n)
         weight = stat_in[i, 12:13, 0:128]
         weight16 = weight.astype(BF16)
-        for p in range(PAIRS):
+        for p in (2 * half, 2 * half + 1):
             cols = slice(p * 128, (p + 1) * 128)
             inner = slice((p % 2) * 128, (p % 2 + 1) * 128)
             kp = pick(k_ref[0:BLK, cols], k_ref[BLK : 2 * BLK, cols], weight16)
             vp = pick(v_ref[0:BLK, cols], v_ref[BLK : 2 * BLK, cols], weight16)
-            qp = stack(qg_in[i, p // 2, 0, :, inner])
-            gp = stack(qg_in[i, p // 2, 1, :, inner])
+            qp = stack(qg_in[i, half, 0, :, inner])
+            gp = stack(qg_in[i, half, 1, :, inner])
             prob = jnp.exp(nt(kp, qp) - stat_in[i, p : p + 1, :]) * stat_in[i, 4 + p : 5 + p, :]
             ds = (prob * (nt(vp, gp) - stat_in[i, 8 + p : 9 + p, :])).astype(BF16)
             dk = nn(ds, qp)
@@ -427,16 +460,12 @@
             dv_acc[BLK : 2 * BLK, cols] += dv * weight
         return carry
 
-    for c in (wins[1, h, r] for h in range(2) for r in range(2)):
+    for c in stats.values():
         c.wait_recv()
-    for a in (0, 1, 3, 2):
-        for b in range(SIDE):
-            slot = a * SIDE + b
-            stats[slot].wait_recv()
-            for half in range(2):
-                if (1, half, slot) in fars:
-                    fars[1, half, slot].wait_recv()
-        lax.fori_loop(a * SIDE, (a + 1) * SIDE, owner_backward, 0)
+    for j in (0, 1, 3, 2):
+        for half in range(2):
+            wait_items(1, half, j)
+            lax.fori_loop(0, SIDE, functools.partial(owner_backward, half, j), 0, unroll=4)
 
     dk_ref[...] = dk_acc[...].astype(BF16)
     dv_ref[...] = dv_acc[...].astype(BF16)
@@ -476,8 +505,8 @@
             pltpu.VMEM((rows, WIDTH), F32),
             dma((2, 3)),
             dma((2, 3)),
-            dma((2, 2, 3, 2)),
-            dma((2, 2, 3, 2)),
+            dma((2, 2, 4, 2)),
+            dma((2, 2, 4, 2)),
             dma((2, 2, 4, 3)),
             dma((2, 2, 4, 3)),
             dma((2, 2, 2)),

time: 100 us -> 84.7 us (0.85)
  Pallas kernels: 95.8 us -> 80.4 us
    pallas_call x1, Pallas kernels: 95.8 us -> 80.4 us  [shards(): pl.pallas_call(kernel, out_shape=[jax.ShapeDtypeStruct((rows, WIDTH), BF1...]
where the time goes in v2:
time: 84.7 us; the launch traced here: 84.5 us
  Pallas kernels  80.4 us (95%)
  local copies, waits for them, and re-layouts  3.46 us (4%)
    pallas_call x1, Pallas kernels, shards(): pl.pallas_call(kernel, out_shape=[jax.ShapeDtypeStruct((rows, WIDTH), BF1...  80.4 us
    unnamed x7, local copies, waits for them, and re-layouts  3.46 us

profile of v2, /device:TPU:0, one launch (start us, length us, event | category | flops | bytes accessed | tf_op | source)
XLA Modules:
  0.0 84.5 jit_solution(4814994245931257969)
XLA Ops:
  0.6 80.4 %shard_map.76 = (bf16[256,512]{1,0:T(8,128)(2,1)}, bf16[256,512]{1,0:T(8,128)(2,1)}, bf16[256,512]{1,0:T(8,128)(2,1)}) custom-call(s32[2,16]{1,0:T(2,128)} %lists_ref.1, bf16[256,512]{1,0:T(8,128)(2,1)} %q_ref.1, bf16[256,512]{1,0:T(8,128)(2,1)} %k_ref.1, bf16[256,512]{1,0:T(8,128)(2,1)} %v_ref.1, bf16[256,512]{1,0:T(8,128)(2,1)} %g_ref.1), custom_call_target="tpu_custom_call" | custom-call | tf_op jit(solution)/shard_map/pallas_call | solution.py:481
  81.1 0.0 copy-start.1
  81.1 1.7 %copy.11 = bf16[256,512]{1,0:T(8,128)(2,1)} copy(bf16[256,512]{1,0:T(8,128)(2,1)} %get-tuple-element.6) | data formatting | bytes 524288
  82.8 0.0 copy-done.1
  82.8 0.0 copy-start
  82.8 0.7 copy.12
  83.5 0.3 copy-done
  83.8 0.7 copy.13
Async XLA Ops:
  81.1 1.7 %copy-start.1 = (bf16[256,512]{1,0:T(8,128)(2,1)S(1)}, bf16[256,512]{1,0:T(8,128)(2,1)}, u32[]{:S(2)}) copy-start(bf16[256,512]{1,0:T(8,128)(2,1)} %get-tuple-element.7) | copy-start | bytes 786436
  82.8 1.0 %copy-start = (bf16[256,512]{1,0:T(8,128)(2,1)S(1)}, bf16[256,512]{1,0:T(8,128)(2,1)}, u32[]{:S(2)}) copy-start(bf16[256,512]{1,0:T(8,128)(2,1)} %get-tuple-element.8) | copy-start | bytes 786436

commit v3 on v2

--- a/solution.py
+++ b/solution.py
@@ -1,5 +1,3 @@
-import functools
-
 import jax
 import jax.numpy as jnp
 from jax import lax
@@ -38,13 +36,17 @@
 
 def kernel(
     lists_ref,
+    q_hbm,
+    k_hbm,
+    v_hbm,
+    g_hbm,
+    dq_ref,
+    dk_ref,
+    dv_ref,
     q_ref,
     k_ref,
     v_ref,
     g_ref,
-    dq_ref,
-    dk_ref,
-    dv_ref,
     qs_ref,
     meta_ref,
     meta_x,
@@ -74,7 +76,14 @@
     win_rs,
     stat_ss,
     stat_rs,
+    load_sem,
 ):
+    loads = []
+    for n, (src, dst) in enumerate(
+        ((k_hbm, k_ref), (v_hbm, v_ref), (q_hbm, q_ref), (g_hbm, g_ref))
+    ):
+        loads.append(pltpu.make_async_copy(src, dst, load_sem.at[n]))
+        loads[n].start()
     me = lax.axis_index("views")
     band = lax.axis_index("sub")
     bands = lax.axis_size("sub")
@@ -107,6 +116,8 @@
     meta_ref[0] = jnp.broadcast_to(found[0][1] + found[1][1], (16, 128))
     meta_ref[1] = jnp.broadcast_to(found[1][0], (16, 128))
     meta_ref[2] = jnp.broadcast_to(found[0][0] + found[1][0], (16, 128))
+    for c in loads:
+        c.wait()
     qs_ref[...] = q_ref[...] * jnp.asarray(0.125, BF16)
 
     pl.semaphore_wait(barrier, 17)
@@ -299,10 +310,11 @@
     def slot_of(half, j, n):
         return j * SIDE + n if half == 0 else n * SIDE + j
 
-    def remote_forward(half, j, n, carry):
+    def remote_forward(half, j, n):
         i = slot_of(half, j, n)
         weight = meta_ref[1, pl.ds(view_of_slot(i), 1), :].astype(BF16)
-        weight = weight * jnp.where(i == 0, 0.0, 1.0).astype(BF16)
+        if i == 0:
+            weight = weight * 0
         for p in (2 * half, 2 * half + 1):
             cols = slice(p * 128, (p + 1) * 128)
             inner = slice((p % 2) * 128, (p % 2 + 1) * 128)
@@ -314,19 +326,20 @@
                 kv_in[i, half, 0, :, inner],
                 kv_in[i, half, 1, :, inner],
             )
-        return carry
-
-    def wait_items(group, half, j):
-        if j == 0:
-            for arr in range(2):
-                wins[group, half, arr].wait_recv()
-        for n in range(1, SIDE):
-            fars[group, half, slot_of(half, j, n)].wait_recv()
+
+    def wait_items(group, j, n):
+        for half in range(2):
+            if n:
+                fars[group, half, slot_of(half, j, n)].wait_recv()
+            elif j == 0:
+                for arr in range(2):
+                    wins[group, half, arr].wait_recv()
 
     for j in (0, 1, 3, 2):
-        for half in range(2):
-            wait_items(0, half, j)
-            lax.fori_loop(0, SIDE, functools.partial(remote_forward, half, j), 0, unroll=4)
+        for n in (0, 1, 3, 2):
+            wait_items(0, j, n)
+            for half in range(2):
+                remote_forward(half, j, n)
         if j == 1:
             send_far(1, 0)
 
@@ -439,7 +452,7 @@
     lax.fori_loop(0, LOCAL, remote_backward, 0, unroll=2)
     dq_ref[...] = (dq_acc[...] * 0.125).astype(BF16)
 
-    def owner_backward(half, j, n, carry):
+    def owner_backward(half, j, n):
         i = slot_of(half, j, n)
         weight = stat_in[i, 12:13, 0:128]
         weight16 = weight.astype(BF16)
@@ -458,14 +471,14 @@
             dk_acc[BLK : 2 * BLK, cols] += dk * weight
             dv_acc[0:BLK, cols] += dv * (1.0 - weight)
             dv_acc[BLK : 2 * BLK, cols] += dv * weight
-        return carry
 
     for c in stats.values():
         c.wait_recv()
     for j in (0, 1, 3, 2):
-        for half in range(2):
-            wait_items(1, half, j)
-            lax.fori_loop(0, SIDE, functools.partial(owner_backward, half, j), 0, unroll=4)
+        for n in (0, 1, 3, 2):
+            wait_items(1, j, n)
+            for half in range(2):
+                owner_backward(half, j, n)
 
     dk_ref[...] = dk_acc[...].astype(BF16)
     dv_ref[...] = dv_acc[...].astype(BF16)
@@ -480,11 +493,11 @@
     stat_rows = (ENTRIES, PAIRS, HALF)
     return pl.pallas_call(
         kernel,
-        out_shape=[jax.ShapeDtypeStruct((rows, WIDTH), BF16)] * 3,
-        in_specs=[vmem] * 5,
+        out_shape=[pltpu.VMEM((rows, WIDTH), BF16)] * 3,
+        in_specs=[vmem] + [pl.BlockSpec(memory_space=pl.ANY)] * 4,
         out_specs=[vmem] * 3,
         scratch_shapes=[
-            pltpu.VMEM((rows, WIDTH), BF16),
+            *[pltpu.VMEM((rows, WIDTH), BF16)] * 5,
             pltpu.VMEM((3, 16, 128), F32),
             pltpu.VMEM((3, 2, 16, 128), F32),
             pltpu.VMEM((3, 2, 16, 128), F32),
@@ -513,6 +526,7 @@
             dma((2, 2, 2)),
             dma((16,)),
             dma((16,)),
+            dma((4,)),
         ],
         compiler_params=pltpu.CompilerParams(
             collective_id=0, has_side_effects=True, vmem_limit_bytes=60 * 1024 * 1024

time: 84.7 us -> 80.5 us (0.950)
  Pallas kernels: 80.4 us -> 76.8 us
  local copies, waits for them, and re-layouts: 3.46 us -> 2.11 us
    pallas_call x1, Pallas kernels: 80.4 us -> 76.8 us  [shards(): pl.pallas_call(kernel, out_shape=[pltpu.VMEM((rows, WIDTH), BF16)] * 3, i...]
    unnamed x7 -> x3, local copies, waits for them, and re-layouts: 3.46 us -> 2.11 us
where the time goes in v3:
time: 80.5 us; the launch traced here: 79.5 us
  Pallas kernels  76.8 us (95%)
  local copies, waits for them, and re-layouts  2.11 us (3%)
    pallas_call x1, Pallas kernels, shards(): pl.pallas_call(kernel, out_shape=[pltpu.VMEM((rows, WIDTH), BF16)] * 3, i...  76.8 us
    unnamed x3, local copies, waits for them, and re-layouts  2.11 us

profile of v3, /device:TPU:0, one launch (start us, length us, event | category | flops | bytes accessed | tf_op | source)
XLA Modules:
  0.0 79.5 jit_solution(3926876611496330129)
XLA Ops:
  0.6 76.8 %shard_map.76 = (bf16[256,512]{1,0:T(8,128)(2,1)S(1)}, bf16[256,512]{1,0:T(8,128)(2,1)S(1)}, bf16[256,512]{1,0:T(8,128)(2,1)S(1)}) custom-call(s32[2,16]{1,0:T(2,128)} %lists_ref.1, bf16[256,512]{1,0:T(8,128)(2,1)} %q_hbm.1, bf16[256,512]{1,0:T(8,128)(2,1)} %k_hbm.1, bf16[256,512]{1,0:T(8,128)(2,1)} %v_hbm.1, bf16[256,512]{1,0:T(8,128)(2,1)} %g_hbm.1), custom_call_target="tpu_custom_call" | custom-call | tf_op jit(solution)/shard_map/pallas_call | solution.py:494
  77.4 0.7 copy.11
  78.1 0.7 copy.12
  78.8 0.7 copy.13

commit v4 on v3

--- a/solution.py
+++ b/solution.py
@@ -51,6 +51,8 @@
     meta_ref,
     meta_x,
     meta_y,
+    block_out,
+    block_in,
     near,
     stage,
     kv_in,
@@ -77,6 +79,8 @@
     stat_ss,
     stat_rs,
     load_sem,
+    block_ss,
+    block_rs,
 ):
     loads = []
     for n, (src, dst) in enumerate(
@@ -94,13 +98,13 @@
     def view(a, b):
         return lax.rem(x + (a % SIDE), SIDE) * SIDE + lax.rem(y + (b % SIDE), SIDE)
 
-    offsets = [(a, b) for a in range(SIDE) for b in range(SIDE) if (a, b) != (0, 0)]
 
     barrier = pltpu.get_barrier_semaphore()
-    for a, b in offsets:
-        pl.semaphore_signal(
-            barrier, inc=1, device_id={"views": view(a, b)}, device_id_type=MESH
-        )
+    for d in (1, 3, 2):
+        for peer in (view(d, 0), view(0, d)):
+            pl.semaphore_signal(
+                barrier, inc=1, device_id={"views": peer}, device_id_type=MESH
+            )
     for s in (after, ahead):
         pl.semaphore_signal(barrier, inc=1, device_id={"sub": s}, device_id_type=MESH)
 
@@ -120,7 +124,7 @@
         c.wait()
     qs_ref[...] = q_ref[...] * jnp.asarray(0.125, BF16)
 
-    pl.semaphore_wait(barrier, 17)
+    pl.semaphore_wait(barrier, 8)
 
     sent = []
 
@@ -251,7 +255,20 @@
             got = meta_x[d % SIDE - 1, plane, pl.ds(row, 1), :]
         else:
             got = meta_y[d % SIDE - 1, plane, pl.ds(row, 1), :]
-        return got.astype(BF16)
+        return got
+
+    blocks = {}
+    for d in (1, 3, 2):
+        for a in range(SIDE):
+            block_out[d - 1, a : a + 1, :] = meta_of("x", -a, 0, view(0, d))
+        block_out[d - 1, 4:8, :] = jnp.zeros((4, 128), F32)
+        blocks[d] = copy(
+            block_out.at[d - 1],
+            block_in.at[d - 1],
+            block_ss.at[d - 1],
+            block_rs.at[d - 1],
+            views=view(0, d),
+        )
 
     def want(group, half, j, d):
         if group == 0 and half == 0:
@@ -274,7 +291,7 @@
                 if d == 0 and j == 0:
                     continue
                 slot = j * SIDE + d if half == 0 else d * SIDE + j
-                weight = wide(want(group, half, j, d))
+                weight = wide(want(group, half, j, d).astype(BF16))
                 for arr in range(2):
                     if j:
                         first = near[group, half, j - 1, arr, 0:BLK, :]
@@ -384,6 +401,7 @@
     deltas = [
         sum(uses[e][blk] * delta_buf[e] for e in range(ENTRIES)) for blk in range(2)
     ]
+    logs = [tops[blk] - jnp.log(invs[blk]) for blk in range(2)]
     stats = {}
     for e in range(ENTRIES):
         first, second = uses[e]
@@ -391,17 +409,8 @@
         delta_buf[e] = delta
         if e < LOCAL:
             a, b = e // SIDE, e % SIDE
-            stat_out[e, 0:4, :] = (
-                first * tops[0] + second * tops[1] + (1.0 - first - second) * FAR
-            )
-            stat_out[e, 4:8, :] = first * invs[0] + second * invs[1]
-            stat_out[e, 8:12, :] = delta
-            if e:
-                stat_out[e, 12:16, :] = jnp.broadcast_to(
-                    wide(meta_ref[0, pl.ds(view(-a, -b), 1), :]), (4, HALF)
-                )
-            else:
-                stat_out[e, 12:16, :] = jnp.ones((4, HALF), F32)
+            stat_out[e, 0:4, :] = first * logs[0] + second * logs[1] + (1.0 - first - second) * FAR
+            stat_out[e, 4:8, :] = delta
             slot = (-a % SIDE) * SIDE + (-b % SIDE)
             to = {"views": view(-a, -b)} if e else {"sub": ahead}
             stats[slot] = copy(
@@ -454,7 +463,13 @@
 
     def owner_backward(half, j, n):
         i = slot_of(half, j, n)
-        weight = stat_in[i, 12:13, 0:128]
+        a, b = i // SIDE, i % SIDE
+        if i == 0:
+            weight = jnp.ones((1, 128), F32)
+        elif b == 0:
+            weight = meta_of("x", -a, 0, me)
+        else:
+            weight = block_in[b - 1, a : a + 1, :]
         weight16 = weight.astype(BF16)
         for p in (2 * half, 2 * half + 1):
             cols = slice(p * 128, (p + 1) * 128)
@@ -463,8 +478,8 @@
             vp = pick(v_ref[0:BLK, cols], v_ref[BLK : 2 * BLK, cols], weight16)
             qp = stack(qg_in[i, half, 0, :, inner])
             gp = stack(qg_in[i, half, 1, :, inner])
-            prob = jnp.exp(nt(kp, qp) - stat_in[i, p : p + 1, :]) * stat_in[i, 4 + p : 5 + p, :]
-            ds = (prob * (nt(vp, gp) - stat_in[i, 8 + p : 9 + p, :])).astype(BF16)
+            prob = jnp.exp(nt(kp, qp) - stat_in[i, p : p + 1, :])
+            ds = (prob * (nt(vp, gp) - stat_in[i, 4 + p : 5 + p, :])).astype(BF16)
             dk = nn(ds, qp)
             dv = nn(prob.astype(BF16), gp)
             dk_acc[0:BLK, cols] += dk * (1.0 - weight)
@@ -472,7 +487,7 @@
             dv_acc[0:BLK, cols] += dv * (1.0 - weight)
             dv_acc[BLK : 2 * BLK, cols] += dv * weight
 
-    for c in stats.values():
+    for c in (*blocks.values(), *stats.values()):
         c.wait_recv()
     for j in (0, 1, 3, 2):
         for n in (0, 1, 3, 2):
@@ -501,6 +516,8 @@
             pltpu.VMEM((3, 16, 128), F32),
             pltpu.VMEM((3, 2, 16, 128), F32),
             pltpu.VMEM((3, 2, 16, 128), F32),
+            pltpu.VMEM((3, 8, 128), F32),
+            pltpu.VMEM((3, 8, 128), F32),
             pltpu.VMEM((2, 2, 3, 2, rows, HALF), BF16),
             pltpu.VMEM((2, 2, 4, 3, 2, BLK, HALF), BF16),
             pltpu.VMEM((16, 2, 2, BLK, HALF), BF16),
@@ -511,8 +528,8 @@
             pltpu.VMEM(stat_rows, F32),
             pltpu.VMEM(stat_rows, F32),
             pltpu.VMEM(stat_rows, F32),
-            pltpu.VMEM((16, 16, HALF), F32),
-            pltpu.VMEM((16, 16, HALF), F32),
+            pltpu.VMEM((16, 8, HALF), F32),
+            pltpu.VMEM((16, 8, HALF), F32),
             pltpu.VMEM((rows, WIDTH), F32),
             pltpu.VMEM((rows, WIDTH), F32),
             pltpu.VMEM((rows, WIDTH), F32),
@@ -527,6 +544,8 @@
             dma((16,)),
             dma((16,)),
             dma((4,)),
+            dma((3,)),
+            dma((3,)),
         ],
         compiler_params=pltpu.CompilerParams(
             collective_id=0, has_side_effects=True, vmem_limit_bytes=60 * 1024 * 1024

time: 80.5 us -> 79.1 us (0.983)
  Pallas kernels: 76.8 us -> 75.3 us
    pallas_call x1, Pallas kernels: 76.8 us -> 75.3 us  [shards(): pl.pallas_call(kernel, out_shape=[pltpu.VMEM((rows, WIDTH), BF16)] * 3, i...]
where the time goes in v4:
time: 79.1 us; the launch traced here: 78 us
  Pallas kernels  75.3 us (95%)
  local copies, waits for them, and re-layouts  2.11 us (3%)
    pallas_call x1, Pallas kernels, shards(): pl.pallas_call(kernel, out_shape=[pltpu.VMEM((rows, WIDTH), BF16)] * 3, i...  75.3 us
    unnamed x3, local copies, waits for them, and re-layouts  2.11 us

profile of v4, /device:TPU:0, one launch (start us, length us, event | category | flops | bytes accessed | tf_op | source)
XLA Modules:
  0.0 78.0 jit_solution(1785645009090201102)
XLA Ops:
  0.6 75.3 %shard_map.76 = (bf16[256,512]{1,0:T(8,128)(2,1)S(1)}, bf16[256,512]{1,0:T(8,128)(2,1)S(1)}, bf16[256,512]{1,0:T(8,128)(2,1)S(1)}) custom-call(s32[2,16]{1,0:T(2,128)} %lists_ref.1, bf16[256,512]{1,0:T(8,128)(2,1)} %q_hbm.1, bf16[256,512]{1,0:T(8,128)(2,1)} %k_hbm.1, bf16[256,512]{1,0:T(8,128)(2,1)} %v_hbm.1, bf16[256,512]{1,0:T(8,128)(2,1)} %g_hbm.1), custom_call_target="tpu_custom_call" | custom-call | tf_op jit(solution)/shard_map/pallas_call | solution.py:509
  75.9 0.7 copy.11
  76.6 0.7 copy.12
  77.3 0.7 copy.13

commit v5 on v4

--- a/solution.py
+++ b/solution.py
@@ -35,7 +35,7 @@
 
 
 def kernel(
-    lists_ref,
+    lists_hbm,
     q_hbm,
     k_hbm,
     v_hbm,
@@ -43,6 +43,7 @@
     dq_ref,
     dk_ref,
     dv_ref,
+    lists_ref,
     q_ref,
     k_ref,
     v_ref,
@@ -84,7 +85,13 @@
 ):
     loads = []
     for n, (src, dst) in enumerate(
-        ((k_hbm, k_ref), (v_hbm, v_ref), (q_hbm, q_ref), (g_hbm, g_ref))
+        (
+            (lists_hbm, lists_ref),
+            (k_hbm, k_ref),
+            (v_hbm, v_ref),
+            (q_hbm, q_ref),
+            (g_hbm, g_ref),
+        )
     ):
         loads.append(pltpu.make_async_copy(src, dst, load_sem.at[n]))
         loads[n].start()
@@ -98,7 +105,6 @@
     def view(a, b):
         return lax.rem(x + (a % SIDE), SIDE) * SIDE + lax.rem(y + (b % SIDE), SIDE)
 
-
     barrier = pltpu.get_barrier_semaphore()
     for d in (1, 3, 2):
         for peer in (view(d, 0), view(0, d)):
@@ -108,6 +114,7 @@
     for s in (after, ahead):
         pl.semaphore_signal(barrier, inc=1, device_id={"sub": s}, device_id_type=MESH)
 
+    loads[0].wait()
     lists = lists_ref[...]
     views = lax.broadcasted_iota(jnp.int32, (16, 16), 0)
     found = []
@@ -120,7 +127,7 @@
     meta_ref[0] = jnp.broadcast_to(found[0][1] + found[1][1], (16, 128))
     meta_ref[1] = jnp.broadcast_to(found[1][0], (16, 128))
     meta_ref[2] = jnp.broadcast_to(found[0][0] + found[1][0], (16, 128))
-    for c in loads:
+    for c in loads[1:]:
         c.wait()
     qs_ref[...] = q_ref[...] * jnp.asarray(0.125, BF16)
 
@@ -242,8 +249,6 @@
                 v_ref[k_rows, cols],
             )
         return carry
-
-    lax.fori_loop(0, 3, local_forward, 0)
 
     for c in metas.values():
         c.wait_recv()
@@ -315,6 +320,7 @@
                     )
 
     send_far(0, 0)
+    lax.fori_loop(0, 3, local_forward, 0)
     pass_on(0)
     send_far(0, 1)
     send_far(0, 3)
@@ -397,7 +403,8 @@
             delta_buf[e, p : p + 1, :] = jnp.sum(rounded * grad_buf[e, p], axis=0, keepdims=True)
         return carry
 
-    lax.fori_loop(0, ENTRIES, delta_part, 0)
+    lax.fori_loop(0, LOCAL, delta_part, 0, unroll=4)
+    lax.fori_loop(LOCAL, ENTRIES, delta_part, 0, unroll=3)
     deltas = [
         sum(uses[e][blk] * delta_buf[e] for e in range(ENTRIES)) for blk in range(2)
     ]
@@ -458,7 +465,7 @@
         return carry
 
     send_far(1, 2)
-    lax.fori_loop(0, LOCAL, remote_backward, 0, unroll=2)
+    lax.fori_loop(0, LOCAL, remote_backward, 0, unroll=4)
     dq_ref[...] = (dq_acc[...] * 0.125).astype(BF16)
 
     def owner_backward(half, j, n):
@@ -509,9 +516,10 @@
     return pl.pallas_call(
         kernel,
         out_shape=[pltpu.VMEM((rows, WIDTH), BF16)] * 3,
-        in_specs=[vmem] + [pl.BlockSpec(memory_space=pl.ANY)] * 4,
+        in_specs=[pl.BlockSpec(memory_space=pl.ANY)] * 5,
         out_specs=[vmem] * 3,
         scratch_shapes=[
+            pltpu.VMEM((2, 16), jnp.int32),
             *[pltpu.VMEM((rows, WIDTH), BF16)] * 5,
             pltpu.VMEM((3, 16, 128), F32),
             pltpu.VMEM((3, 2, 16, 128), F32),
@@ -543,7 +551,7 @@
             dma((2, 2, 2)),
             dma((16,)),
             dma((16,)),
-            dma((4,)),
+            dma((5,)),
             dma((3,)),
             dma((3,)),
         ],

time: 79.1 us -> 78.1 us (0.987)
  Pallas kernels: 75.3 us -> 74.4 us
    pallas_call x1, Pallas kernels: 75.3 us -> 74.4 us  [shards(): pl.pallas_call(kernel, out_shape=[pltpu.VMEM((rows, WIDTH), BF16)] * 3, i...]
where the time goes in v5:
time: 78.1 us; the launch traced here: 77.2 us
  Pallas kernels  74.4 us (95%)
  local copies, waits for them, and re-layouts  2.11 us (3%)
    pallas_call x1, Pallas kernels, shards(): pl.pallas_call(kernel, out_shape=[pltpu.VMEM((rows, WIDTH), BF16)] * 3, i...  74.4 us
    unnamed x3, local copies, waits for them, and re-layouts  2.11 us

profile of v5, /device:TPU:0, one launch (start us, length us, event | category | flops | bytes accessed | tf_op | source)
XLA Modules:
  0.0 77.2 jit_solution(1865506011124356298)
XLA Ops:
  0.6 74.4 %shard_map.76 = (bf16[256,512]{1,0:T(8,128)(2,1)S(1)}, bf16[256,512]{1,0:T(8,128)(2,1)S(1)}, bf16[256,512]{1,0:T(8,128)(2,1)S(1)}) custom-call(s32[2,16]{1,0:T(2,128)} %lists_hbm.1, bf16[256,512]{1,0:T(8,128)(2,1)} %q_hbm.1, bf16[256,512]{1,0:T(8,128)(2,1)} %k_hbm.1, bf16[256,512]{1,0:T(8,128)(2,1)} %v_hbm.1, bf16[256,512]{1,0:T(8,128)(2,1)} %g_hbm.1), custom_call_target="tpu_custom_call" | custom-call | tf_op jit(solution)/shard_map/pallas_call | solution.py:516
  75.0 0.7 copy.11
  75.8 0.7 copy.12
  76.5 0.7 copy.13

commit v6 on v5

--- a/solution.py
+++ b/solution.py
@@ -40,9 +40,7 @@
     k_hbm,
     v_hbm,
     g_hbm,
-    dq_ref,
-    dk_ref,
-    dv_ref,
+    out_ref,
     lists_ref,
     q_ref,
     k_ref,
@@ -127,10 +125,6 @@
     meta_ref[0] = jnp.broadcast_to(found[0][1] + found[1][1], (16, 128))
     meta_ref[1] = jnp.broadcast_to(found[1][0], (16, 128))
     meta_ref[2] = jnp.broadcast_to(found[0][0] + found[1][0], (16, 128))
-    for c in loads[1:]:
-        c.wait()
-    qs_ref[...] = q_ref[...] * jnp.asarray(0.125, BF16)
-
     pl.semaphore_wait(barrier, 8)
 
     sent = []
@@ -165,6 +159,8 @@
             views=view(0, -d),
         )
 
+    for c in loads[1:3]:
+        c.wait()
     own = ((k_ref, v_ref), (qs_ref, g_ref))
     nears = {}
 
@@ -212,8 +208,9 @@
                 )
 
     send_near(0)
-    send_window(0)
-    send_window(1)
+    for c in loads[3:]:
+        c.wait()
+    qs_ref[...] = q_ref[...] * jnp.asarray(0.125, BF16)
 
     lane = lax.broadcasted_iota(jnp.int32, (1, 128), 1)
     low = jnp.where(lane < 64, 1.0, 0.0)
@@ -320,7 +317,9 @@
                     )
 
     send_far(0, 0)
-    lax.fori_loop(0, 3, local_forward, 0)
+    send_window(0)
+    send_window(1)
+    lax.fori_loop(0, 3, local_forward, 0, unroll=3)
     pass_on(0)
     send_far(0, 1)
     send_far(0, 3)
@@ -450,7 +449,7 @@
             dv_acc[k_rows, cols] += nn(prob.astype(BF16), stack(g_ref[q_rows, cols]))
         return carry
 
-    lax.fori_loop(0, 3, local_backward, 0)
+    lax.fori_loop(0, 3, local_backward, 0, unroll=3)
 
     def remote_backward(i, carry):
         weight = meta_ref[1, pl.ds(view_of_slot(i), 1), :]
@@ -466,7 +465,7 @@
 
     send_far(1, 2)
     lax.fori_loop(0, LOCAL, remote_backward, 0, unroll=4)
-    dq_ref[...] = (dq_acc[...] * 0.125).astype(BF16)
+    out_ref[0] = (dq_acc[...] * 0.125).astype(BF16)
 
     def owner_backward(half, j, n):
         i = slot_of(half, j, n)
@@ -502,8 +501,8 @@
             for half in range(2):
                 owner_backward(half, j, n)
 
-    dk_ref[...] = dk_acc[...].astype(BF16)
-    dv_ref[...] = dv_acc[...].astype(BF16)
+    out_ref[1] = dk_acc[...].astype(BF16)
+    out_ref[2] = dv_acc[...].astype(BF16)
     for c in sent:
         c.wait_send()
 
@@ -513,11 +512,11 @@
     rows = 2 * BLK
     dma = pltpu.SemaphoreType.DMA
     stat_rows = (ENTRIES, PAIRS, HALF)
-    return pl.pallas_call(
+    out = pl.pallas_call(
         kernel,
-        out_shape=[pltpu.VMEM((rows, WIDTH), BF16)] * 3,
+        out_shape=pltpu.VMEM((3, rows, WIDTH), BF16),
         in_specs=[pl.BlockSpec(memory_space=pl.ANY)] * 5,
-        out_specs=[vmem] * 3,
+        out_specs=vmem,
         scratch_shapes=[
             pltpu.VMEM((2, 16), jnp.int32),
             *[pltpu.VMEM((rows, WIDTH), BF16)] * 5,
@@ -559,6 +558,7 @@
             collective_id=0, has_side_effects=True, vmem_limit_bytes=60 * 1024 * 1024
         ),
     )(block_lists, queries, keys, values, out_grad)
+    return out[0], out[1], out[2]
 
 
 def solution(mesh):

time: 78.1 us -> 76.7 us (0.982)
  local copies, waits for them, and re-layouts: 2.11 us -> 0.89 us
    unnamed x3 -> x0, local copies, waits for them, and re-layouts: 2.11 us -> none
    squeeze x0 -> x1, local copies, waits for them, and re-layouts: none -> 0.89 us  [shards(): return (out[0], out[1], out[2])]
where the time goes in v6:
time: 76.7 us; the launch traced here: 75.9 us
  Pallas kernels  74.4 us (97%)
  local copies, waits for them, and re-layouts  0.89 us (1%)
    pallas_call x1, Pallas kernels, shards(): pl.pallas_call(kernel, out_shape=pltpu.VMEM((3, rows, WIDTH), BF16), in_s...  74.4 us

profile of v6, /device:TPU:0, one launch (start us, length us, event | category | flops | bytes accessed | tf_op | source)
XLA Modules:
  0.0 75.9 jit_solution(12151840959637273844)
XLA Ops:
  0.6 74.4 %shard_map.76 = bf16[3,256,512]{2,1,0:T(8,128)(2,1)S(1)} custom-call(s32[2,16]{1,0:T(2,128)} %lists_hbm.1, bf16[256,512]{1,0:T(8,128)(2,1)} %q_hbm.1, bf16[256,512]{1,0:T(8,128)(2,1)} %k_hbm.1, bf16[256,512]{1,0:T(8,128)(2,1)} %v_hbm.1, bf16[256,512]{1,0:T(8,128)(2,1)} %g_hbm.1), custom_call_target="tpu_custom_call" | custom-call | tf_op jit(solution)/shard_map/pallas_call | solution.py:515
  75.0 0.9 %slice_bitcast_fusion = (bf16[256,512]{1,0:T(8,128)(2,1)}, bf16[256,512]{1,0:T(8,128)(2,1)}, bf16[256,512]{1,0:T(8,128)(2,1)}) fusion(bf16[3,256,512]{2,1,0:T(8,128)(2,1)S(1)} %shard_map.76), kind=kLoop, calls=%fused_computation | loop fusion | bytes 1572864 | tf_op jit(solution)/shard_map/squeeze | solution.py:561

commit v7 on v6

--- a/solution.py
+++ b/solution.py
@@ -259,19 +259,6 @@
             got = meta_y[d % SIDE - 1, plane, pl.ds(row, 1), :]
         return got
 
-    blocks = {}
-    for d in (1, 3, 2):
-        for a in range(SIDE):
-            block_out[d - 1, a : a + 1, :] = meta_of("x", -a, 0, view(0, d))
-        block_out[d - 1, 4:8, :] = jnp.zeros((4, 128), F32)
-        blocks[d] = copy(
-            block_out.at[d - 1],
-            block_in.at[d - 1],
-            block_ss.at[d - 1],
-            block_rs.at[d - 1],
-            views=view(0, d),
-        )
-
     def want(group, half, j, d):
         if group == 0 and half == 0:
             return meta_of("y", d, 0, view(-j, 0))
@@ -325,6 +312,18 @@
     send_far(0, 3)
     send_far(0, 2)
     send_near(1)
+    blocks = {}
+    for d in (1, 3, 2):
+        for a in range(SIDE):
+            block_out[d - 1, a : a + 1, :] = meta_of("x", -a, 0, view(0, d))
+        block_out[d - 1, 4:8, :] = jnp.zeros((4, 128), F32)
+        blocks[d] = copy(
+            block_out.at[d - 1],
+            block_in.at[d - 1],
+            block_ss.at[d - 1],
+            block_rs.at[d - 1],
+            views=view(0, d),
+        )
 
     def view_of_slot(i):
         return lax.rem(x + SIDE - i // SIDE, SIDE) * SIDE + lax.rem(y + SIDE - i % SIDE, SIDE)
@@ -364,6 +363,8 @@
                 remote_forward(half, j, n)
         if j == 1:
             send_far(1, 0)
+
+    pass_on(1)
 
     has_prev = jnp.where(band > 0, 1.0, 0.0)
     ones = jnp.full((1, HALF), 1.0, F32)
@@ -423,7 +424,6 @@
                 stat_out.at[e], stat_in.at[slot], stat_ss.at[slot], stat_rs.at[slot], **to
             )
 
-    pass_on(1)
     send_far(1, 1)
     send_far(1, 3)
 

time: 76.7 us -> 76.3 us (level)
  no operation moved by 1% of the time
where the time goes in v7:
time: 76.3 us; the launch traced here: 76 us
  Pallas kernels  74.4 us (98%)
  local copies, waits for them, and re-layouts  0.89 us (1%)
    pallas_call x1, Pallas kernels, shards(): pl.pallas_call(kernel, out_shape=pltpu.VMEM((3, rows, WIDTH), BF16), in_s...  74.4 us

profile of v7, /device:TPU:0, one launch (start us, length us, event | category | flops | bytes accessed | tf_op | source)
XLA Modules:
  0.0 76.0 jit_solution(11351535886133947797)
XLA Ops:
  0.6 74.4 %shard_map.76 = bf16[3,256,512]{2,1,0:T(8,128)(2,1)S(1)} custom-call(s32[2,16]{1,0:T(2,128)} %lists_hbm.1, bf16[256,512]{1,0:T(8,128)(2,1)} %q_hbm.1, bf16[256,512]{1,0:T(8,128)(2,1)} %k_hbm.1, bf16[256,512]{1,0:T(8,128)(2,1)} %v_hbm.1, bf16[256,512]{1,0:T(8,128)(2,1)} %g_hbm.1), custom_call_target="tpu_custom_call" | custom-call | tf_op jit(solution)/shard_map/pallas_call | solution.py:515
  75.1 0.9 %slice_bitcast_fusion = (bf16[256,512]{1,0:T(8,128)(2,1)}, bf16[256,512]{1,0:T(8,128)(2,1)}, bf16[256,512]{1,0:T(8,128)(2,1)}) fusion(bf16[3,256,512]{2,1,0:T(8,128)(2,1)S(1)} %shard_map.76), kind=kLoop, calls=%fused_computation | loop fusion | bytes 1572864 | tf_op jit(solution)/shard_map/squeeze | solution.py:561
